TPU v7x, 128 devices: a whole 4x4x4 slice. The times are simulated.
128 devices in a mesh: inner: 32 (over y, x_hi, z), outer: 4 (over x_lo, core).
Axes of the slice: x: 4 (x_hi: 2, x_lo: 2; x = x_hi * 2 + x_lo), y: 4, z: 4, core: 2. Of those that a mesh axis runs over, the one named last changes fastest.
Arguments:
- design: bfloat16 [1048576, 128], P(('inner', 'outer')), may hold values from -6 to 6
- sign_bits: int32 [1048576], P(('inner', 'outer')), may hold values from 0 to 1
- sampled: int32 [131072], P(('inner', 'outer')), may hold values from 0 to 8191
- owner_map: int32 [131072, 1], P(('inner', 'outer')), may hold values from 0 to 127; in each aligned block of 1024 rows (0 to 1023, 1024 to 2047, ...) at most 16 rows name the same one
Outputs:
- sketch_tiles: float32 [128, 128, 16, 128], P(('inner', 'outer'))
Inputs may be any that keep to these rules, and one draw needn't show every extreme that they name: `owner_map`: among the 1024 samples of one block no owner appears more than 16 times, and some owner appears exactly 16 times.
All inputs are finite; a program needn't handle non-finite values.
Results may differ from a plain program's by a relative error of at most 0.0003.
Values sent between devices are 32-bit elements; how exact they have to be, the bound alone decides.
No kernel may reach another device: no remote copies, remote signals or barrier semaphores. Data moves between devices by JAX's collectives and lax.ppermute only.
A program may use at most 64 MiB of HBM per device.

v0:
```python
import math

import jax
import jax.numpy as jnp
from jax import lax
from jax.sharding import PartitionSpec as P

LANES = 128


def partner_2(value, axis, bit):
    mask = 2**bit
    pairs = [(source, source ^ mask) for source in range(lax.axis_size(axis))]
    return lax.ppermute(value, axis, pairs)


def hadamard(order):
    left_index = jnp.arange(order, dtype=jnp.int32)[:, None]
    right_index = jnp.arange(order, dtype=jnp.int32)[None, :]
    common_bits = jnp.bitwise_and(left_index, right_index)
    parity_sum = jnp.zeros((order, order), jnp.int32)
    for bit_number in range(max(order.bit_length() - 1, 0)):
        parity_sum = parity_sum + jnp.bitwise_and(jnp.right_shift(common_bits, bit_number), 1)
    return (1 - 2 * jnp.bitwise_and(parity_sum, 1)).astype(jnp.float32)


def slot_positions(owner_block, devices):
    one_hot = (
        owner_block[:, :, None] == jnp.arange(devices, dtype=jnp.int32)[None, None, :]
    ).astype(jnp.int32)
    running = jnp.cumsum(one_hot, axis=1) - 1
    return jnp.sum(one_hot * running, axis=2)


def outer_sections(values):
    my_outer = lax.axis_index("outer")
    for bit_number in range(lax.axis_size("outer").bit_length() - 1):
        partner = partner_2(values, "outer", bit_number)
        upper = jnp.bitwise_and(jnp.right_shift(my_outer, bit_number), 1) == 1
        values = jnp.where(upper, partner - values, values + partner)
    return values


def per_device(design, sign_bits, sampled, owner_map):
    n_inner = lax.axis_size("inner")
    n_outer = lax.axis_size("outer")
    devices = n_inner * n_outer
    local_rows, columns = design.shape
    blocks = local_rows // LANES
    highest = lax.Precision.HIGHEST
    flipped = jnp.where(sign_bits[:, None] == 1, design, -design).reshape(blocks, LANES, columns)
    section_one = jnp.einsum(
        "ab,bjc->ajc",
        hadamard(blocks).astype(jnp.bfloat16),
        flipped,
        preferred_element_type=jnp.float32,
    )
    mixed = jnp.einsum("jk,akc->ajc", hadamard(LANES), section_one, precision=highest).reshape(
        local_rows, columns
    )
    my_inner = lax.axis_index("inner")
    for bit_number in range(n_inner.bit_length() - 1):
        partner = partner_2(mixed, "inner", bit_number)
        upper = jnp.bitwise_and(jnp.right_shift(my_inner, bit_number), 1) == 1
        mixed = jnp.where(upper, partner - mixed, mixed + partner)
    mixed = outer_sections(mixed)
    samples_here = sampled.shape[0]
    picked = mixed[sampled] * (1.0 / math.sqrt(samples_here * devices))
    owners = owner_map[:, 0]
    position = slot_positions(owners[None, :], devices)[0]
    capacity = 2 * samples_here // devices
    outgoing = jnp.zeros((devices * capacity, columns), jnp.float32)
    outgoing = (
        outgoing.at[owners * capacity + position].set(picked).reshape(devices, capacity, columns)
    )
    arrived = lax.all_to_all(outgoing, ("inner", "outer"), split_axis=0, concat_axis=0, tiled=True)
    return arrived[None]


def solution(mesh):
    in_specs = (
        P(("inner", "outer"), None),
        P(("inner", "outer")),
        P(("inner", "outer")),
        P(("inner", "outer"), None),
    )
    out_specs = P(("inner", "outer"), None, None, None)
    return jax.shard_map(
        per_device, mesh=mesh, in_specs=in_specs, out_specs=out_specs, check_vma=False
    )
```

profile of v0, /device:TPU:1, one launch (start us, length us, event | category | flops | bytes accessed | tf_op | source)
XLA Modules:
  0.0 657.9 jit_solution(10707885090979776546)
XLA Ops:
  0.0 0.8 broadcast_compare_fusion
  0.8 5.8 negate_select_fusion
  6.6 1.7 fusion.2
  8.3 9.0 %fusion = f32[64,128,128]{1,2,0:T(8,128)} fusion(f32[64,128,128]{2,0,1:T(8,128)S(1)} %fusion.2), kind=kOutput, calls=%fused_computation.2 | convolution fusion | flops 1611022336 | bytes 8388608 | tf_op jit(solution)/shard_map/jk,akc->ajc/dot_general | solution.py:58
  17.3 2.5 collective-permute-start
  19.8 90.6 %collective-permute-done = f32[8192,128]{1,0:T(8,128)} collective-permute-done((f32[8192,128]{1,0:T(8,128)}, f32[8192,128]{1,0:T(8,128)}, u32[]{:S(2)}, u32[]{:S(2)}) %collective-permute-start) | collective-permute-done | bytes 4194336 | tf_op jit(solution)/shard_map/ppermute | solution.py:14
  110.3 5.8 add_select_fusion.6
  116.2 3.1 collective-permute-start.1
  119.3 89.7 %collective-permute-done.1 = f32[8192,128]{1,0:T(8,128)} collective-permute-done((f32[8192,128]{1,0:T(8,128)}, f32[8192,128]{1,0:T(8,128)}, u32[]{:S(2)}, u32[]{:S(2)}) %collective-permute-start.1) | collective-permute-done | bytes 4194336 | tf_op jit(solution)/shard_map/ppermute | solution.py:14
  208.9 5.8 add_select_fusion.5
  214.8 2.7 collective-permute-start.2
  217.5 88.9 %collective-permute-done.2 = f32[8192,128]{1,0:T(8,128)} collective-permute-done((f32[8192,128]{1,0:T(8,128)}, f32[8192,128]{1,0:T(8,128)}, u32[]{:S(2)}, u32[]{:S(2)}) %collective-permute-start.2) | collective-permute-done | bytes 4194336 | tf_op jit(solution)/shard_map/ppermute | solution.py:14
  306.5 5.8 add_select_fusion.4
  312.3 1.3 collective-permute-start.3
  313.6 88.0 %collective-permute-done.3 = f32[8192,128]{1,0:T(8,128)} collective-permute-done((f32[8192,128]{1,0:T(8,128)}, f32[8192,128]{1,0:T(8,128)}, u32[]{:S(2)}, u32[]{:S(2)}) %collective-permute-start.3) | collective-permute-done | bytes 4194336 | tf_op jit(solution)/shard_map/ppermute | solution.py:14
  401.6 5.8 add_select_fusion.3
  407.4 2.9 collective-permute-start.4
  410.3 86.9 %collective-permute-done.4 = f32[8192,128]{1,0:T(8,128)} collective-permute-done((f32[8192,128]{1,0:T(8,128)}, f32[8192,128]{1,0:T(8,128)}, u32[]{:S(2)}, u32[]{:S(2)}) %collective-permute-start.4) | collective-permute-done | bytes 4194336 | tf_op jit(solution)/shard_map/ppermute | solution.py:14
  497.2 5.8 add_select_fusion.2
  503.1 5.0 collective-permute-start.5
  508.0 0.0 copy-start
  508.0 7.1 %collective-permute-done.5 = f32[8192,128]{1,0:T(8,128)} collective-permute-done((f32[8192,128]{1,0:T(8,128)}, f32[8192,128]{1,0:T(8,128)}, u32[]{:S(2)}, u32[]{:S(2)}) %collective-permute-start.5) | collective-permute-done | bytes 4194336 | tf_op jit(solution)/shard_map/ppermute | solution.py:14
  515.2 5.8 add_select_fusion.1
  521.0 0.0 copy-start.1
  521.0 1.2 collective-permute-start.6
  522.2 0.0 copy-done
  522.2 0.2 fusion.9
  522.4 0.3 fusion.5
  522.7 0.1 copy.6
  522.9 0.4 fusion.4
  523.3 0.0 copy-done.1
  523.3 89.7 %collective-permute-done.6 = f32[8192,128]{1,0:T(8,128)} collective-permute-done((f32[8192,128]{1,0:T(8,128)}, f32[8192,128]{1,0:T(8,128)}, u32[]{:S(2)}, u32[]{:S(2)}) %collective-permute-start.6) | collective-permute-done | bytes 4194336 | tf_op jit(solution)/shard_map/ppermute | solution.py:14
  613.1 5.8 add_select_fusion
  618.9 9.2 %scatter_custom_fusion = f32[2048,128]{1,0:T(8,128)S(1)} fusion(s32[1024]{0:T(1024)S(1)} %bitcast.38, f32[]{:T(128)} %constant.16.clone.1, f32[]{:T(128)} %constant.8.clone.1, f32[8192,128]{1,0:T(8,128)} %add_select_fusion, s32[1024]{0:T(1024)S(1)} %fusion.55), kind=kCustom, calls=%fused_computation.19 | custom fusion | flops 131072 | bytes 5246984 | tf_op jit(solution)/shard_map/scatter | solution.py:74
  628.1 28.9 %all_to_all.5 = f32[128,16,128]{2,1,0:T(8,128)S(1)} all-to-all(f32[128,16,128]{2,1,0:T(8,128)S(1)} %bitcast.32), channel_id=1, replica_groups=mesh['inner'=32,'outer'=4] {'inner','outer'}, dimensions={0} | all-to-all | bytes 2097152 | tf_op jit(solution)/shard_map/all_to_all | solution.py:76
  657.0 1.0 copy.16
  (6 shorter events, 0.1 us)
Async XLA Ops:
  17.3 93.1 %collective-permute-start = (f32[8192,128]{1,0:T(8,128)}, f32[8192,128]{1,0:T(8,128)}, u32[]{:S(2)}, u32[]{:S(2)}) collective-permute-start(f32[8192,128]{1,0:T(8,128)} %bitcast.14), channel_id=1, source_target_pairs={{0,4},{4,0},{8,12},{12,8},{16,20},{20,16},{24,28},{28,24},{32,36},... | collective-permute-start | bytes 12582920 | tf_op jit(solution)/shard_map/ppermute | solution.py:14
  116.2 92.8 %collective-permute-start.1 = (f32[8192,128]{1,0:T(8,128)}, f32[8192,128]{1,0:T(8,128)}, u32[]{:S(2)}, u32[]{:S(2)}) collective-permute-start(f32[8192,128]{1,0:T(8,128)} %add_select_fusion.6), channel_id=1, source_target_pairs={{0,8},{4,12},{8,0},{12,4},{16,24},{20,28},{24,16},{28,20},{32,40},... | collective-permute-start | bytes 12582920 | tf_op jit(solution)/shard_map/ppermute | solution.py:14
  214.8 91.7 %collective-permute-start.2 = (f32[8192,128]{1,0:T(8,128)}, f32[8192,128]{1,0:T(8,128)}, u32[]{:S(2)}, u32[]{:S(2)}) collective-permute-start(f32[8192,128]{1,0:T(8,128)} %add_select_fusion.5), channel_id=1, source_target_pairs={{0,16},{4,20},{8,24},{12,28},{16,0},{20,4},{24,8},{28,12},{32,48},... | collective-permute-start | bytes 12582920 | tf_op jit(solution)/shard_map/ppermute | solution.py:14
  312.3 89.3 %collective-permute-start.3 = (f32[8192,128]{1,0:T(8,128)}, f32[8192,128]{1,0:T(8,128)}, u32[]{:S(2)}, u32[]{:S(2)}) collective-permute-start(f32[8192,128]{1,0:T(8,128)} %add_select_fusion.4), channel_id=1, source_target_pairs={{0,32},{4,36},{8,40},{12,44},{16,48},{20,52},{24,56},{28,60},{32,0... | collective-permute-start | bytes 12582920 | tf_op jit(solution)/shard_map/ppermute | solution.py:14
  407.4 89.9 %collective-permute-start.4 = (f32[8192,128]{1,0:T(8,128)}, f32[8192,128]{1,0:T(8,128)}, u32[]{:S(2)}, u32[]{:S(2)}) collective-permute-start(f32[8192,128]{1,0:T(8,128)} %add_select_fusion.3), channel_id=1, source_target_pairs={{0,64},{4,68},{8,72},{12,76},{16,80},{20,84},{24,88},{28,92},{32,9... | collective-permute-start | bytes 12582920 | tf_op jit(solution)/shard_map/ppermute | solution.py:14
  503.1 12.1 %collective-permute-start.5 = (f32[8192,128]{1,0:T(8,128)}, f32[8192,128]{1,0:T(8,128)}, u32[]{:S(2)}, u32[]{:S(2)}) collective-permute-start(f32[8192,128]{1,0:T(8,128)} %add_select_fusion.2), channel_id=1, source_target_pairs={{0,1},{1,0},{2,3},{3,2},{4,5},{5,4},{6,7},{7,6},{8,9},{9,8},{10,11... | collective-permute-start | bytes 12582920 | tf_op jit(solution)/shard_map/ppermute | solution.py:14
  508.0 14.2 %copy-start = (s32[1024,1]{0,1:T(1,128)S(1)}, s32[1024,1]{0,1:T(1,128)}, u32[]{:S(2)}) copy-start(s32[1024,1]{0,1:T(1,128)} %param.7) | copy-start | bytes 12292
  521.0 2.3 copy-start.1
  521.0 92.1 %collective-permute-start.6 = (f32[8192,128]{1,0:T(8,128)}, f32[8192,128]{1,0:T(8,128)}, u32[]{:S(2)}, u32[]{:S(2)}) collective-permute-start(f32[8192,128]{1,0:T(8,128)} %add_select_fusion.1), channel_id=1, source_target_pairs={{0,2},{1,3},{2,0},{3,1},{4,6},{5,7},{6,4},{7,5},{8,10},{9,11},{10,... | collective-permute-start | bytes 12582920 | tf_op jit(solution)/shard_map/ppermute | solution.py:14
where the time goes:
time: 658 us
  waiting for transfers between devices  541 us (82%)
  other arithmetic  57.5 us (9%)
  blocking collectives  28.9 us (4%)
  starting transfers between devices  18.7 us (3%)
  matrix products  10.7 us (2%)
    ppermute x7, waiting for transfers between devices, partner_2(): return lax.ppermute(value, axis, pairs)  541 us
    select_n x5, other arithmetic, per_device(): mixed = jnp.where(upper, partner - mixed, mixed + partner)  29.1 us
    all_to_all x1, blocking collectives, per_device(): lax.all_to_all(outgoing, ('inner', 'outer'), split_axis=0, concat_axis=0,...  28.9 us
    ppermute x7, starting transfers between devices, partner_2(): return lax.ppermute(value, axis, pairs)  18.7 us
  transfers between devices with their start and end apart: 7, of which 7 were waited for; matrix products, arithmetic and copies ran while one was open for 0% of the time, Pallas kernels for 0%

commit v1 on v0

v1 whole, which is shorter than its diff:
```python
import math

import jax
import jax.numpy as jnp
from jax import lax
from jax.experimental import pallas as pl
from jax.experimental.pallas import tpu as pltpu
from jax.sharding import PartitionSpec as P

AXES = ("inner", "outer")
DEVICES = 128
COLS = 128
LANES = 128
BLOCKS = 64
ROWS = BLOCKS * LANES
SAMPLED = 1024
CAP = 16
DATA = BLOCKS + CAP
SCALE = 1.0 / math.sqrt(SAMPLED * DEVICES)
LIMIT = 48 * 1024 * 1024


def sylvester(rows, columns):
    common = lax.broadcasted_iota(jnp.int32, (rows, columns), 0) & lax.broadcasted_iota(
        jnp.int32, (rows, columns), 1
    )
    common = common ^ (common >> 4)
    common = common ^ (common >> 2)
    common = common ^ (common >> 1)
    return (1 - 2 * (common & 1)).astype(jnp.float32)


def butterflies(values):
    half = 1
    while half < len(values):
        for start in range(0, len(values), 2 * half):
            for i in range(start, start + half):
                a, b = values[i], values[i + half]
                values[i], values[i + half] = a + b, a - b
        half *= 2
    return values


def table_kernel(sampled_ref, owner_ref, out_ref, at_slot, named):
    sampled = sampled_ref[...] + 1
    owners = owner_ref[...]
    one_hot = lax.broadcasted_iota(jnp.int32, (DEVICES, SAMPLED), 0) == owners
    one_hot16 = one_hot.astype(jnp.float32).astype(jnp.bfloat16)
    upto = (
        lax.broadcasted_iota(jnp.int32, (SAMPLED, SAMPLED), 0)
        <= lax.broadcasted_iota(jnp.int32, (SAMPLED, SAMPLED), 1)
    )
    running = jnp.dot(
        one_hot16,
        upto.astype(jnp.float32).astype(jnp.bfloat16),
        preferred_element_type=jnp.float32,
    )
    position = jnp.sum(jnp.where(one_hot, running, 0.0), axis=0, keepdims=True) - 1.0
    slots = lax.broadcasted_iota(jnp.int32, (DEVICES, SAMPLED), 0)
    at_slot[...] = jnp.where(slots == position.astype(jnp.int32), 1.0, 0.0)
    table = jnp.zeros((DEVICES, DEVICES), jnp.float32)
    for part, weight in ((sampled >> 7, 128.0), (sampled & 127, 1.0)):
        named[...] = jnp.where(one_hot, part.astype(jnp.float32), 0.0)
        table = table + weight * lax.dot_general(
            at_slot[...].astype(jnp.bfloat16),
            named[...].astype(jnp.bfloat16),
            (((1,), (1,)), ((), ())),
            preferred_element_type=jnp.float32,
        )
    out_ref[...] = table[:CAP]


def local_kernel(design_ref, signs_ref, table_ref, out_ref, mixed):
    table = table_ref[...]
    order = 2 * LANES
    matrix = sylvester(order, order)

    @pl.loop(0, BLOCKS // 2)
    def _(pair):
        signs = (2 * signs_ref[pl.ds(2 * pair, 2), :] - 1).astype(jnp.float32)
        signed = jnp.concatenate(
            [matrix[:, :LANES] * signs[0:1], matrix[:, LANES:] * signs[1:2]], axis=1
        ).astype(jnp.bfloat16)
        rows = pl.ds(pl.multiple_of(pair * order, order), order)
        mixed[rows, :] = jnp.dot(
            signed, design_ref[rows, :], preferred_element_type=jnp.float32
        )

    @pl.loop(0, order // 8)
    def _(slab):
        places = [
            pl.ds(pl.multiple_of(pair * order + slab * 8, 8), 8) for pair in range(BLOCKS // 2)
        ]
        for place, value in zip(places, butterflies([mixed[place, :] for place in places])):
            mixed[place, :] = value

    for block in range(BLOCKS):
        out_ref[pl.ds(block, COLS, stride=DATA), :] = mixed[
            block * LANES : (block + 1) * LANES, :
        ].T

    @pl.loop(0, COLS)
    def _(column):
        out_ref[pl.ds(pl.multiple_of(column * DATA + BLOCKS, 8), CAP), :] = table


def pick_kernel(column_ref, out_ref, mixed, picked):
    matrix = sylvester(DEVICES, DEVICES).astype(jnp.bfloat16)
    matrix = jnp.concatenate([matrix, matrix], axis=1)

    @pl.loop(0, BLOCKS // 2)
    def _(pair):
        high, low = [], []
        for t in range(2):
            values = column_ref[pl.ds(2 * pair + t, DEVICES, stride=DATA), :]
            top = values.astype(jnp.bfloat16)
            high.append(top)
            low.append((values - top.astype(jnp.float32)).astype(jnp.bfloat16))
        operand = jnp.concatenate(
            [jnp.concatenate(high, axis=1), jnp.concatenate(low, axis=1)], axis=0
        )
        result = jnp.dot(matrix, operand, preferred_element_type=jnp.float32)
        for t in range(2):
            rows = pl.ds(pl.multiple_of((2 * pair + t) * DEVICES, DEVICES), DEVICES)
            mixed[rows, :] = result[:, t * LANES : (t + 1) * LANES]

    @pl.loop(0, DEVICES)
    def _(source):
        table = column_ref[pl.ds(pl.multiple_of(source * DATA + BLOCKS, 8), CAP), :]
        named = table.astype(jnp.int32) - 1
        lanes = [named[t * 8 : (t + 1) * 8] & (LANES - 1) for t in range(2)]
        blocks = [named[t * 8 : (t + 1) * 8] >> 7 for t in range(2)]
        bits = [[(b >> n) & 1 == 1 for n in range(6)] for b in blocks]

        def choose(first, level):
            if level == 0:
                row = jnp.broadcast_to(
                    mixed[pl.ds(first * DEVICES + source, 1), :], (8, LANES)
                )
                return [jnp.take_along_axis(row, lane, axis=1) for lane in lanes]
            lower = choose(first, level - 1)
            upper = choose(first + (1 << (level - 1)), level - 1)
            return [
                jnp.where(bits[t][level - 1], upper[t], lower[t]) for t in range(2)
            ]

        found = choose(0, 6)
        for t in range(2):
            rows = pl.ds(pl.multiple_of(source * CAP + t * 8, 8), 8)
            picked[rows, :] = jnp.where(blocks[t] >= 0, found[t] * SCALE, 0.0)

    for group in range(CAP):
        out_ref[pl.ds(group, DEVICES, stride=CAP), :] = picked[
            group * LANES : (group + 1) * LANES, :
        ].T


def turn_kernel(arrived_ref, out_ref):
    for group in range(CAP):
        out_ref[group * LANES : (group + 1) * LANES, :] = arrived_ref[
            pl.ds(group, COLS, stride=CAP), :
        ].T


def call(kernel, rows, *args, scratch=()):
    vmem = pl.BlockSpec(memory_space=pltpu.VMEM)
    return pl.pallas_call(
        kernel,
        out_shape=jax.ShapeDtypeStruct((rows, LANES), jnp.float32),
        in_specs=[vmem] * len(args),
        out_specs=vmem,
        scratch_shapes=[pltpu.VMEM(shape, jnp.float32) for shape in scratch],
        compiler_params=pltpu.CompilerParams(vmem_limit_bytes=LIMIT),
    )(*args)


def exchange(values):
    values = values.reshape(DEVICES, -1, LANES)
    return lax.all_to_all(values, AXES, split_axis=0, concat_axis=0, tiled=True).reshape(
        -1, LANES
    )


def per_device(design, sign_bits, sampled, owner_map):
    table = call(
        table_kernel,
        CAP,
        sampled.reshape(1, SAMPLED),
        owner_map.reshape(1, SAMPLED),
        scratch=((DEVICES, SAMPLED), (DEVICES, SAMPLED)),
    )
    columns = call(
        local_kernel,
        COLS * DATA,
        design,
        sign_bits.reshape(BLOCKS, LANES),
        table,
        scratch=((ROWS, LANES),),
    )
    columns = exchange(columns)
    picked = call(pick_kernel, DEVICES * CAP, columns, scratch=((ROWS, LANES), (DEVICES * CAP, LANES)))
    picked = exchange(picked)
    tiles = call(turn_kernel, DEVICES * CAP, picked)
    return tiles.reshape(1, DEVICES, CAP, COLS)


def solution(mesh):
    in_specs = (
        P(AXES, None),
        P(AXES),
        P(AXES),
        P(AXES, None),
    )
    out_specs = P(AXES, None, None, None)
    return jax.shard_map(
        per_device, mesh=mesh, in_specs=in_specs, out_specs=out_specs, check_vma=False
    )
```

time: 658 us -> 157 us (0.24)
  waiting for transfers between devices: 541 us -> 0 us
  blocking collectives: 28.9 us -> 102 us
  other arithmetic: 57.5 us -> 0 us
  Pallas kernels: 0 us -> 50.3 us
  starting transfers between devices: 18.7 us -> 0 us
  matrix products: 10.7 us -> 0 us
    ppermute x7 -> x0, waiting for transfers between devices: 541 us -> none  [partner_2(): return lax.ppermute(value, axis, pairs)]
    all_to_all x1 -> x2, blocking collectives: 28.9 us -> 102 us  [exchange(): lax.all_to_all(values, AXES, split_axis=0, concat_axis=0, tiled=True)]
    pallas_call x0 -> x4, Pallas kernels: none -> 50.3 us  [call(): pl.pallas_call(kernel, out_shape=jax.ShapeDtypeStruct((rows, LANES), jnp....]
    select_n x9 -> x0, other arithmetic: 46.6 us -> none  [the longest x5 29.1 us: per_device(): mixed = jnp.where(upper, partner - mixed, mixed + partner)]
    ppermute x7 -> x0, starting transfers between devices: 18.7 us -> none  [partner_2(): return lax.ppermute(value, axis, pairs)]
    dot_general x2 -> x0, matrix products: 10.7 us -> none  [the longest x1 8.98 us: per_device(): jnp.einsum('jk,akc->ajc', hadamard(LANES), section_one, precision=highest)]
    scatter x1 -> x0, other arithmetic: 9.15 us -> none  [per_device(): outgoing.at[owners * capacity + position].set(picked)]
  transfers between devices with their start and end apart: 7 -> 0, of which waited for: 7 -> 0; matrix products, arithmetic and copies ran while one was open for 0% -> 0% of each run, Pallas kernels for 0% -> 0%
where the time goes in v1:
time: 157 us; the launch traced here: 156 us
  blocking collectives  102 us (65%)
  Pallas kernels  50.3 us (32%)
  local copies, waits for them, and re-layouts  3.72 us (2%)
    all_to_all x2, blocking collectives, exchange(): lax.all_to_all(values, AXES, split_axis=0, concat_axis=0, tiled=True)  102 us
    pallas_call x4, Pallas kernels, call(): pl.pallas_call(kernel, out_shape=jax.ShapeDtypeStruct((rows, LANES), jnp....  50.3 us
    unnamed x8, local copies, waits for them, and re-layouts  3.72 us

profile of v1, /device:TPU:1, one launch (start us, length us, event | category | flops | bytes accessed | tf_op | source)
XLA Modules:
  0.0 156.3 jit_solution(6654690562027525356)
XLA Ops:
  0.0 0.0 copy-start.2
  0.0 0.7 copy-done.2
  0.7 0.0 copy-start.3
  0.7 0.7 copy-done.3
  1.4 0.6 shard_map.46.table_ref
  2.0 0.0 copy-start
  2.0 1.6 %copy-done = bf16[8192,128]{1,0:T(8,128)(2,1)S(1)} copy-done((bf16[8192,128]{1,0:T(8,128)(2,1)S(1)}, bf16[8192,128]{1,0:T(8,128)(2,1)}, u32[]{:S(2)}) %copy-start) | copy-done | bytes 2097176
  3.6 0.0 copy-start.1
  3.6 0.8 copy-done.1
  4.4 11.5 %shard_map.47 = f32[10240,128]{1,0:T(8,128)} custom-call(bf16[8192,128]{1,0:T(8,128)(2,1)S(1)} %copy-done, s32[64,128]{1,0:T(8,128)S(1)} %bitcast.10, f32[16,128]{1,0:T(8,128)S(1)} %shard_map.46.table_ref), custom_call_target="tpu_custom_call" | custom-call | tf_op jit(solution)/shard_map/pallas_call | solution.py:167
  15.9 76.0 %all_to_all.10 = f32[128,80,128]{2,1,0:T(8,128)} all-to-all(f32[128,80,128]{2,1,0:T(8,128)} %bitcast.13), channel_id=1, replica_groups=mesh['inner'=32,'outer'=4] {'inner','outer'}, dimensions={0} | all-to-all | bytes 10485760 | tf_op jit(solution)/shard_map/all_to_all | solution.py:179
  91.9 36.7 %shard_map.48 = f32[2048,128]{1,0:T(8,128)S(1)} custom-call(f32[10240,128]{1,0:T(8,128)} %bitcast.14), custom_call_target="tpu_custom_call" | custom-call | tf_op jit(solution)/shard_map/pallas_call | solution.py:167
  128.7 26.3 %all_to_all.11 = f32[128,16,128]{2,1,0:T(8,128)S(1)} all-to-all(f32[128,16,128]{2,1,0:T(8,128)S(1)} %bitcast.9), channel_id=1, replica_groups=mesh['inner'=32,'outer'=4] {'inner','outer'}, dimensions={0} | all-to-all | bytes 2097152 | tf_op jit(solution)/shard_map/all_to_all | solution.py:179
  154.9 1.3 shard_map.49
Async XLA Ops:
  0.0 0.7 copy-start.2
  0.7 0.7 copy-start.3
  2.0 1.6 %copy-start = (bf16[8192,128]{1,0:T(8,128)(2,1)S(1)}, bf16[8192,128]{1,0:T(8,128)(2,1)}, u32[]{:S(2)}) copy-start(bf16[8192,128]{1,0:T(8,128)(2,1)} %design_ref.1) | copy-start | bytes 6291460
  3.6 0.8 copy-start.1

commit v2 on v1

v2 whole, which is shorter than its diff:
```python
import math

import jax
import jax.numpy as jnp
from jax import lax
from jax.experimental import pallas as pl
from jax.experimental.pallas import tpu as pltpu
from jax.sharding import PartitionSpec as P

AXES = ("inner", "outer")
DEVICES = 128
COLS = 128
LANES = 128
BLOCKS = 64
ROWS = BLOCKS * LANES
SAMPLED = 1024
CAP = 16
LISTED = SAMPLED // LANES
TABLE = LISTED + CAP
SCALE = 1.0 / math.sqrt(SAMPLED * DEVICES)
PARTS = 8
F32 = jnp.float32
BF16 = jnp.bfloat16


def iota(shape, axis):
    return lax.broadcasted_iota(jnp.int32, shape, axis)


def sylvester(rows, columns):
    common = iota((rows, columns), 0) & iota((rows, columns), 1)
    common = common ^ (common >> 4)
    common = common ^ (common >> 2)
    common = common ^ (common >> 1)
    return (1 - 2 * (common & 1)).astype(F32)


def butterflies(values):
    half = 1
    while half < len(values):
        for start in range(0, len(values), 2 * half):
            for i in range(start, start + half):
                a, b = values[i], values[i + half]
                values[i], values[i + half] = a + b, a - b
        half *= 2
    return values


def transform_in_place(ref, places):
    for place, value in zip(places, butterflies([ref[place, :] for place in places])):
        ref[place, :] = value


def aligned(start, size):
    return pl.ds(pl.multiple_of(start, 8), size)


def table_kernel(sampled_ref, owner_ref, out_ref, at_slot, named):
    owners = owner_ref[...]
    one_hot = iota((DEVICES, SAMPLED), 0) == owners
    upto = iota((SAMPLED, SAMPLED), 0) <= iota((SAMPLED, SAMPLED), 1)
    running = jnp.dot(
        one_hot.astype(F32).astype(BF16), upto.astype(F32).astype(BF16), preferred_element_type=F32
    )
    position = jnp.sum(jnp.where(one_hot, running, 0.0), axis=0, keepdims=True) - 1.0
    at_slot[...] = jnp.where(
        iota((DEVICES, SAMPLED), 0) == position.astype(jnp.int32), 1.0, 0.0
    )
    place = iota((1, SAMPLED), 1) + 1
    table = jnp.zeros((DEVICES, DEVICES), F32)
    for part, weight in ((place >> 7, 128.0), (place & 127, 1.0)):
        named[...] = jnp.where(one_hot, part.astype(F32), 0.0)
        table = table + weight * lax.dot_general(
            at_slot[...].astype(BF16),
            named[...].astype(BF16),
            (((1,), (1,)), ((), ())),
            preferred_element_type=F32,
        )
    for row in range(LISTED):
        out_ref[row : row + 1, :] = sampled_ref[:, row * LANES : (row + 1) * LANES].astype(F32)
    out_ref[LISTED:, :] = table[:CAP]


def local_kernel(design_hbm, signs_hbm, out_ref, design, signs, mixed, turned, sems, sign_sem):
    chunk = ROWS // PARTS
    copies = [
        pltpu.make_async_copy(
            design_hbm.at[pl.ds(n * chunk, chunk)], design.at[pl.ds(n * chunk, chunk)], sems.at[n]
        )
        for n in range(PARTS)
    ]
    sign_copy = pltpu.make_async_copy(signs_hbm, signs, sign_sem)
    sign_copy.start()
    for copy in copies:
        copy.start()
    order = 2 * LANES
    pairs = BLOCKS // 2
    matrix = sylvester(order, order)
    sign_copy.wait()
    for n in range(PARTS):
        copies[n].wait()
        for pair in range(n * pairs // PARTS, (n + 1) * pairs // PARTS):
            sign = (2 * signs[2 * pair : 2 * pair + 2, :] - 1).astype(F32)
            signed = jnp.concatenate(
                [matrix[:, :LANES] * sign[0:1], matrix[:, LANES:] * sign[1:2]], axis=1
            ).astype(BF16)
            rows = pl.ds(pair * order, order)
            mixed[rows, :] = jnp.dot(signed, design[rows, :], preferred_element_type=F32)

    @pl.loop(0, order // 8)
    def _(slab):
        transform_in_place(
            mixed, [aligned(pair * order + slab * 8, 8) for pair in range(pairs)]
        )

    for block in range(BLOCKS):
        rows = slice(block * LANES, (block + 1) * LANES)
        turned[rows, :] = mixed[rows, :].T

    @pl.loop(0, COLS, unroll=4)
    def _(column):
        for part in range(BLOCKS // 8):
            out_ref[aligned(column * BLOCKS + part * 8, 8), :] = turned[
                pl.ds(part * 8 * COLS + column, 8, stride=COLS), :
            ]


def gather_rows(parts):
    row = iota((8, LANES), 0)
    step = 1
    while len(parts) > 1:
        upper = (row & step) != 0
        parts = [
            jnp.where(upper, b, a) + pltpu.roll(jnp.where(upper, a, b), step, 0)
            for a, b in zip(parts[0::2], parts[1::2])
        ]
        step *= 2
    return parts[0]


def pick_kernel(column_hbm, table_ref, out_ref, mixed, found, picked, sems):
    copies = [
        pltpu.make_async_copy(
            column_hbm.at[:, pl.ds(8 * n, 8), :], mixed.at[:, pl.ds(8 * n, 8), :], sems.at[n]
        )
        for n in range(PARTS)
    ]
    for copy in copies:
        copy.start()
    for n in range(PARTS):
        copies[n].wait()
        rows = pl.ds(8 * n, 8)

        @pl.loop(0, 8)
        def _(low):
            places = [high * 8 + low for high in range(16)]
            values = butterflies([mixed[place, rows, :] for place in places])
            for place, value in zip(places, values):
                mixed[place, rows, :] = value

        @pl.loop(0, 16)
        def _(high):
            places = [high * 8 + low for low in range(8)]
            values = butterflies([mixed[place, rows, :] for place in places])
            for place, value in zip(places, values):
                mixed[place, rows, :] = value

    half = BLOCKS // 2
    place = iota((2 * LANES, LANES), 0).astype(F32).astype(BF16)
    row8 = iota((8, LANES), 0)
    one, zero = jnp.ones((), BF16), jnp.zeros((), BF16)

    @pl.loop(0, DEVICES, unroll=2)
    def _(source):
        listed = table_ref[aligned(source * TABLE, LISTED), :].astype(jnp.int32)
        key = ((listed & (LANES - 1)) + ((listed >> 12) << 7)).astype(F32)
        block = (listed >> 7) & (half - 1)
        values = mixed[source]
        top = values.astype(BF16)
        rest = (values - top.astype(F32)).astype(BF16)
        operand = jnp.concatenate(
            [
                jnp.concatenate([top[:half], top[half:]], axis=1),
                jnp.concatenate([rest[:half], rest[half:]], axis=1),
            ],
            axis=0,
        )
        one_hot = jnp.concatenate(
            [
                jnp.where(
                    place == jnp.broadcast_to(key[r : r + 1], (2 * LANES, LANES)).astype(BF16),
                    one,
                    zero,
                )
                for r in range(LISTED)
            ],
            axis=1,
        )
        result = jnp.dot(operand, one_hot, preferred_element_type=F32)
        result = result[:half] + result[half:]
        parts = []
        for r in range(LISTED):
            wanted = jnp.broadcast_to(block[r : r + 1], (8, LANES))
            part = jnp.zeros((8, LANES), F32)
            for g in range(half // 8):
                part = jnp.where(
                    wanted == row8 + 8 * g,
                    result[8 * g : 8 * g + 8, r * LANES : (r + 1) * LANES],
                    part,
                )
            parts.append(part)
        found = gather_rows(parts)

        slots = table_ref[aligned(source * TABLE + LISTED, CAP), :].astype(jnp.int32) - 1
        for t in range(2):
            slot = slots[8 * t : 8 * t + 8]
            lane = slot & (LANES - 1)
            rows = [
                jnp.take_along_axis(jnp.broadcast_to(found[r : r + 1], (8, LANES)), lane, axis=1)
                for r in range(LISTED)
            ]
            for n in range(3):
                odd = (slot >> (7 + n)) & 1 == 1
                rows = [jnp.where(odd, b, a) for a, b in zip(rows[0::2], rows[1::2])]
            picked[aligned(source * CAP + 8 * t, 8), :] = jnp.where(
                slot >= 0, rows[0] * SCALE, 0.0
            )

    for group in range(CAP):
        out_ref[pl.ds(group, DEVICES, stride=CAP), :] = picked[
            group * LANES : (group + 1) * LANES, :
        ].T


def turn_kernel(arrived_ref, out_ref):
    for group in range(CAP):
        out_ref[group * LANES : (group + 1) * LANES, :] = arrived_ref[
            pl.ds(group, COLS, stride=CAP), :
        ].T


HBM = pl.BlockSpec(memory_space=pl.ANY)
VMEM = pl.BlockSpec(memory_space=pltpu.VMEM)


def call(kernel, rows, specs, *args, scratch=(), limit=24):
    return pl.pallas_call(
        kernel,
        out_shape=jax.ShapeDtypeStruct((rows, LANES), F32),
        in_specs=specs,
        out_specs=VMEM,
        scratch_shapes=scratch,
        compiler_params=pltpu.CompilerParams(vmem_limit_bytes=limit * 1024 * 1024),
    )(*args)


def exchange(values):
    values = values.reshape(DEVICES, -1, LANES)
    return lax.all_to_all(values, AXES, split_axis=0, concat_axis=0, tiled=True)


def gather_tables(table):
    inner = lax.axis_size("inner")
    near = [[g * 4 + i for i in range(4)] for g in range(inner // 4)]
    far = [[g + 4 * i for i in range(inner // 4)] for g in range(4)]
    table = lax.all_gather(table, "outer", axis=0, tiled=True)
    table = lax.all_gather(table, "inner", axis=0, tiled=True, axis_index_groups=near)
    return lax.all_gather(table, "inner", axis=0, tiled=True, axis_index_groups=far)


def per_device(design, sign_bits, sampled, owner_map):
    vmem, dma = pltpu.VMEM, pltpu.SemaphoreType.DMA
    table = call(
        table_kernel,
        TABLE,
        [VMEM, VMEM],
        sampled.reshape(1, SAMPLED),
        owner_map.reshape(1, SAMPLED),
        scratch=[vmem((DEVICES, SAMPLED), F32), vmem((DEVICES, SAMPLED), F32)],
    )
    tables = gather_tables(table)
    columns = call(
        local_kernel,
        COLS * BLOCKS,
        [HBM, HBM],
        design,
        sign_bits.reshape(BLOCKS, LANES),
        scratch=[
            vmem((ROWS, LANES), BF16),
            vmem((BLOCKS, LANES), jnp.int32),
            vmem((ROWS, LANES), F32),
            vmem((ROWS, LANES), F32),
            dma((PARTS,)),
            dma(()),
        ],
    )
    picked = call(
        pick_kernel,
        DEVICES * CAP,
        [HBM, VMEM],
        exchange(columns),
        tables,
        scratch=[
            vmem((DEVICES, BLOCKS, LANES), F32),
            vmem((8, LANES), F32),
            vmem((DEVICES * CAP, LANES), F32),
            dma((PARTS,)),
        ],
    )
    tiles = call(turn_kernel, DEVICES * CAP, [VMEM], exchange(picked).reshape(-1, LANES))
    return tiles.reshape(1, DEVICES, CAP, COLS)


def solution(mesh):
    in_specs = (
        P(AXES, None),
        P(AXES),
        P(AXES),
        P(AXES, None),
    )
    out_specs = P(AXES, None, None, None)
    return jax.shard_map(
        per_device, mesh=mesh, in_specs=in_specs, out_specs=out_specs, check_vma=False
    )
```

time: 157 us -> 209 us (1.33)
  waiting for transfers between devices: 0 us -> 51.7 us
  blocking collectives: 102 us -> 84.8 us
  between operations: 0.03 us -> 13.5 us
  starting transfers between devices: 0 us -> 12 us
  Pallas kernels: 50.3 us -> 40.4 us
    all_to_all x2 -> x1, blocking collectives: 102 us -> 26.7 us  [exchange(): return lax.all_to_all(values, AXES, split_axis=0, concat_axis=0, tiled=True)]
    all_gather x0 -> x2, blocking collectives: none -> 58.1 us  [the longest x1 47.1 us: gather_tables(): table = lax.all_gather(table, 'outer', axis=0, tiled=True)]
    all_gather x0 -> x1, waiting for transfers between devices: none -> 51.7 us  [gather_tables(): lax.all_gather(table, 'inner', axis=0, tiled=True, axis_index_groups=far)]
    all_to_all x0 -> x1, starting transfers between devices: none -> 12 us  [exchange(): return lax.all_to_all(values, AXES, split_axis=0, concat_axis=0, tiled=True)]
    pallas_call x4, Pallas kernels: 50.3 us -> 40.4 us  [call(): pl.pallas_call(kernel, out_shape=jax.ShapeDtypeStruct((rows, LANES), F32)...]
    unnamed x8 -> x12, local copies, waits for them, and re-layouts: 3.72 us -> 5.73 us
  transfers between devices with their start and end apart: 0 -> 2, of which waited for: 0 -> 1; matrix products, arithmetic and copies ran while one was open for 0% -> 0% of each run, Pallas kernels for 0% -> 0%
where the time goes in v2:
time: 209 us; the launch traced here: 208 us
  blocking collectives  84.8 us (41%)
  waiting for transfers between devices  51.7 us (25%)
  Pallas kernels  40.4 us (19%)
  between operations  13.5 us (6%)
  starting transfers between devices  12 us (6%)
  local copies, waits for them, and re-layouts  5.73 us (3%)
    all_gather x1, waiting for transfers between devices, gather_tables(): lax.all_gather(table, 'inner', axis=0, tiled=True, axis_index_groups=far)  51.7 us
    all_gather x1, blocking collectives, gather_tables(): table = lax.all_gather(table, 'outer', axis=0, tiled=True)  47.1 us
    pallas_call x4, Pallas kernels, call(): pl.pallas_call(kernel, out_shape=jax.ShapeDtypeStruct((rows, LANES), F32)...  40.4 us
    all_to_all x1, blocking collectives, exchange(): return lax.all_to_all(values, AXES, split_axis=0, concat_axis=0, tiled=True)  26.7 us
    all_to_all x1, starting transfers between devices, exchange(): return lax.all_to_all(values, AXES, split_axis=0, concat_axis=0, tiled=True)  12 us
    all_gather x1, blocking collectives, gather_tables(): lax.all_gather(table, 'inner', axis=0, tiled=True, axis_index_groups=near)  11 us
    unnamed x12, local copies, waits for them, and re-layouts  5.73 us
  transfers between devices with their start and end apart: 2, of which 1 were waited for; matrix products, arithmetic and copies ran while one was open for 0% of the time, Pallas kernels for 0%

profile of v2, /device:TPU:1, one launch (start us, length us, event | category | flops | bytes accessed | tf_op | source)
XLA Modules:
  0.0 208.2 jit_solution(3165221811769788997)
XLA Ops:
  6.5 0.0 copy-start.1
  6.5 1.6 copy-done.1
  8.1 0.0 copy-start.3
  8.1 0.8 copy-done.3
  8.9 8.0 %shard_map.46 = f32[8192,128]{1,0:T(8,128)S(1)} custom-call(bf16[8192,128]{1,0:T(8,128)(2,1)S(1)} %copy-done.1, s32[64,128]{1,0:T(8,128)S(1)} %bitcast.10), custom_call_target="tpu_custom_call" | custom-call | tf_op jit(solution)/shard_map/pallas_call | solution.py:247
  16.9 0.0 copy-start
  16.9 2.0 copy-done
  18.9 0.0 copy-start.4
  18.9 0.0 copy-start.5
  18.9 12.0 %all-to-all-start = ((f32[128,64,128]{2,1,0:T(8,128)}), f32[128,64,128]{2,1,0:T(8,128)}, u32[]{:S(2)}, u32[]{:S(2)}) async-start(f32[128,64,128]{2,1,0:T(8,128)} %bitcast.7), calls=%async_computation | async-start | bytes 8388608 | tf_op jit(solution)/shard_map/all_to_all | solution.py:259
  30.9 0.0 all-gather.2.cloned.1.call-start
  30.9 0.0 copy-done.4
  30.9 0.0 copy-done.5
  30.9 0.7 shard_map.47
  31.6 47.1 %all_gather.9 = f32[96,128]{1,0:T(8,128)S(1)} all-gather(f32[24,128]{1,0:T(8,128)S(1)} %shard_map.47), channel_id=1, replica_groups=mesh['inner'=32,'outer'=4] {'outer'}, dimensions={0}, use_global_device_ids=true | all-gather | bytes 61440 | tf_op jit(solution)/shard_map/all_gather | solution.py:266
  78.7 11.0 %all_gather.10 = f32[384,128]{1,0:T(8,128)} all-gather(f32[96,128]{1,0:T(8,128)S(1)} %all_gather.9), channel_id=1, replica_groups={{0,4,8,12},{16,20,24,28},{32,36,40,44},{48,52,56,60},{64,68,72,76},{80,..., dimensions={0}, use_global_device_ids=true | all-gather | bytes 245760 | tf_op jit(solution)/shard_map/all_gather | solution.py:267
  89.7 0.0 all-gather.2.cloned.1.call-update
  89.7 51.7 %all-gather.2.cloned.1.call-done.table_ref = f32[3072,128]{1,0:T(8,128)} async-done(((f32[384,128]{1,0:T(8,128)}), f32[3072,128]{1,0:T(8,128)}) %all-gather.2.cloned.1.call-update) | async-done | bytes 1572880 | tf_op jit(solution)/shard_map/all_gather | solution.py:268
  141.4 0.0 all-to-all-done.column_hbm
  141.5 0.0 copy-start.2
  141.5 1.4 copy-done.2
  142.9 30.4 %shard_map.48 = f32[2048,128]{1,0:T(8,128)S(1)} custom-call(f32[128,64,128]{2,1,0:T(8,128)} %all-to-all-done.column_hbm, f32[3072,128]{1,0:T(8,128)S(1)} %copy-done.2), custom_call_target="tpu_custom_call" | custom-call | tf_op jit(solution)/shard_map/pallas_call | solution.py:247
  173.3 26.7 %all_to_all.10 = f32[128,16,128]{2,1,0:T(8,128)S(1)} all-to-all(f32[128,16,128]{2,1,0:T(8,128)S(1)} %bitcast.9), channel_id=1, replica_groups=mesh['inner'=32,'outer'=4] {'inner','outer'}, dimensions={0} | all-to-all | bytes 2097152 | tf_op jit(solution)/shard_map/all_to_all | solution.py:259
  200.0 1.3 shard_map.49
Async XLA Ops:
  6.5 1.6 copy-start.1
  8.1 0.8 copy-start.3
  16.9 2.0 copy-start
  18.9 12.0 %copy-start.4 = (s32[1024]{0:T(1024)S(1)}, s32[1024]{0:T(1024)}, u32[]{:S(2)}) copy-start(s32[1024]{0:T(1024)} %param.6) | copy-start | bytes 12292
  18.9 12.0 %copy-start.5 = (s32[1024,1]{0,1:T(1,128)S(1)}, s32[1024,1]{0,1:T(1,128)}, u32[]{:S(2)}) copy-start(s32[1024,1]{0,1:T(1,128)} %param.7) | copy-start | bytes 12292
  18.9 122.5 %all-to-all-start = ((f32[128,64,128]{2,1,0:T(8,128)}), f32[128,64,128]{2,1,0:T(8,128)}, u32[]{:S(2)}, u32[]{:S(2)}) async-start(f32[128,64,128]{2,1,0:T(8,128)} %bitcast.7), calls=%async_computation | async-start | bytes 8388608 | tf_op jit(solution)/shard_map/all_to_all | solution.py:259
  30.9 110.6 %all-gather.2.cloned.1.call-start = ((), (), s32[]{:S(2)}) async-start(), calls=%async_computation.2 | async-start | bytes 1769472 | tf_op jit(solution)/shard_map/all_gather | solution.py:268
  141.5 1.4 copy-start.2
Sparse Core Ops, SparseCore 0:
  89.9 51.5 all-gather.1

commit v3 on v2

--- a/solution.py
+++ b/solution.py
@@ -19,6 +19,7 @@
 TABLE = LISTED + CAP
 SCALE = 1.0 / math.sqrt(SAMPLED * DEVICES)
 PARTS = 8
+GROUP = 8
 F32 = jnp.float32
 BF16 = jnp.bfloat16
 
@@ -55,8 +56,7 @@
     return pl.ds(pl.multiple_of(start, 8), size)
 
 
-def table_kernel(sampled_ref, owner_ref, out_ref, at_slot, named):
-    owners = owner_ref[...]
+def slot_table(sampled, owners, at_slot, named):
     one_hot = iota((DEVICES, SAMPLED), 0) == owners
     upto = iota((SAMPLED, SAMPLED), 0) <= iota((SAMPLED, SAMPLED), 1)
     running = jnp.dot(
@@ -76,27 +76,35 @@
             (((1,), (1,)), ((), ())),
             preferred_element_type=F32,
         )
-    for row in range(LISTED):
-        out_ref[row : row + 1, :] = sampled_ref[:, row * LANES : (row + 1) * LANES].astype(F32)
-    out_ref[LISTED:, :] = table[:CAP]
-
-
-def local_kernel(design_hbm, signs_hbm, out_ref, design, signs, mixed, turned, sems, sign_sem):
+    listed = [sampled[:, row * LANES : (row + 1) * LANES].astype(F32) for row in range(LISTED)]
+    return jnp.concatenate(listed + [table[:CAP]], axis=0)
+
+
+def local_kernel(
+    design_hbm, signs_hbm, sampled_hbm, owner_hbm, out_ref, table_ref,
+    design, signs, sampled, owners, at_slot, named, mixed, turned, sems, small_sems,
+):
     chunk = ROWS // PARTS
+    small = [
+        pltpu.make_async_copy(source, target, small_sems.at[n])
+        for n, (source, target) in enumerate(
+            ((sampled_hbm, sampled), (owner_hbm, owners), (signs_hbm, signs))
+        )
+    ]
     copies = [
         pltpu.make_async_copy(
             design_hbm.at[pl.ds(n * chunk, chunk)], design.at[pl.ds(n * chunk, chunk)], sems.at[n]
         )
         for n in range(PARTS)
     ]
-    sign_copy = pltpu.make_async_copy(signs_hbm, signs, sign_sem)
-    sign_copy.start()
-    for copy in copies:
+    for copy in small + copies:
         copy.start()
     order = 2 * LANES
     pairs = BLOCKS // 2
     matrix = sylvester(order, order)
-    sign_copy.wait()
+    for copy in small:
+        copy.wait()
+    table_ref[...] = slot_table(sampled[...], owners[...], at_slot, named)
     for n in range(PARTS):
         copies[n].wait()
         for pair in range(n * pairs // PARTS, (n + 1) * pairs // PARTS):
@@ -138,7 +146,8 @@
     return parts[0]
 
 
-def pick_kernel(column_hbm, table_ref, out_ref, mixed, found, picked, sems):
+def pick_kernel(me_ref, column_hbm, table_ref, out_ref, mixed, found, picked, sems):
+    me = me_ref[0]
     copies = [
         pltpu.make_async_copy(
             column_hbm.at[:, pl.ds(8 * n, 8), :], mixed.at[:, pl.ds(8 * n, 8), :], sems.at[n]
@@ -165,58 +174,44 @@
             for place, value in zip(places, values):
                 mixed[place, rows, :] = value
 
-    half = BLOCKS // 2
-    place = iota((2 * LANES, LANES), 0).astype(F32).astype(BF16)
+    place = iota((LANES, LANES), 0).astype(F32).astype(BF16)
     row8 = iota((8, LANES), 0)
     one, zero = jnp.ones((), BF16), jnp.zeros((), BF16)
 
-    @pl.loop(0, DEVICES, unroll=2)
-    def _(source):
-        listed = table_ref[aligned(source * TABLE, LISTED), :].astype(jnp.int32)
-        key = ((listed & (LANES - 1)) + ((listed >> 12) << 7)).astype(F32)
-        block = (listed >> 7) & (half - 1)
+    def pick(source):
+        listed = table_ref[aligned((source ^ me) * TABLE, LISTED), :].astype(jnp.int32)
+        key = (listed & (LANES - 1)).astype(F32)
+        block = listed >> 7
         values = mixed[source]
         top = values.astype(BF16)
-        rest = (values - top.astype(F32)).astype(BF16)
-        operand = jnp.concatenate(
-            [
-                jnp.concatenate([top[:half], top[half:]], axis=1),
-                jnp.concatenate([rest[:half], rest[half:]], axis=1),
-            ],
-            axis=0,
-        )
-        one_hot = jnp.concatenate(
-            [
-                jnp.where(
-                    place == jnp.broadcast_to(key[r : r + 1], (2 * LANES, LANES)).astype(BF16),
-                    one,
-                    zero,
-                )
-                for r in range(LISTED)
-            ],
-            axis=1,
-        )
-        result = jnp.dot(operand, one_hot, preferred_element_type=F32)
-        result = result[:half] + result[half:]
+        operand = jnp.concatenate([top, (values - top.astype(F32)).astype(BF16)], axis=0)
         parts = []
         for r in range(LISTED):
+            mine = jnp.broadcast_to(key[r : r + 1], (16, LANES)).astype(BF16)
+            one_hot = jnp.concatenate(
+                [jnp.where(place[16 * g : 16 * g + 16] == mine, one, zero) for g in range(8)],
+                axis=0,
+            )
+            result = jnp.dot(operand, one_hot, preferred_element_type=F32)
             wanted = jnp.broadcast_to(block[r : r + 1], (8, LANES))
-            part = jnp.zeros((8, LANES), F32)
-            for g in range(half // 8):
-                part = jnp.where(
-                    wanted == row8 + 8 * g,
-                    result[8 * g : 8 * g + 8, r * LANES : (r + 1) * LANES],
-                    part,
-                )
-            parts.append(part)
-        found = gather_rows(parts)
-
-        slots = table_ref[aligned(source * TABLE + LISTED, CAP), :].astype(jnp.int32) - 1
+            values = [
+                result[8 * g : 8 * g + 8] + result[BLOCKS + 8 * g : BLOCKS + 8 * g + 8]
+                for g in range(8)
+            ]
+            for n in range(3, 6):
+                odd = (wanted >> n) & 1 == 1
+                values = [jnp.where(odd, b, a) for a, b in zip(values[0::2], values[1::2])]
+            parts.append(jnp.where(wanted & 7 == row8, values[0], 0.0))
+        found[aligned(source * LISTED, LISTED), :] = gather_rows(parts)
+
+    def place_in_slots(source):
+        slots = table_ref[aligned((source ^ me) * TABLE + LISTED, CAP), :].astype(jnp.int32) - 1
+        here = found[aligned(source * LISTED, LISTED), :]
         for t in range(2):
             slot = slots[8 * t : 8 * t + 8]
             lane = slot & (LANES - 1)
             rows = [
-                jnp.take_along_axis(jnp.broadcast_to(found[r : r + 1], (8, LANES)), lane, axis=1)
+                jnp.take_along_axis(jnp.broadcast_to(here[r : r + 1], (8, LANES)), lane, axis=1)
                 for r in range(LISTED)
             ]
             for n in range(3):
@@ -226,6 +221,18 @@
                 slot >= 0, rows[0] * SCALE, 0.0
             )
 
+    for n in range(GROUP):
+        pick(n)
+
+    @pl.loop(1, DEVICES // GROUP)
+    def _(group):
+        for n in range(GROUP):
+            place_in_slots((group - 1) * GROUP + n)
+            pick(group * GROUP + n)
+
+    for n in range(GROUP):
+        place_in_slots(DEVICES - GROUP + n)
+
     for group in range(CAP):
         out_ref[pl.ds(group, DEVICES, stride=CAP), :] = picked[
             group * LANES : (group + 1) * LANES, :
@@ -241,73 +248,87 @@
 
 HBM = pl.BlockSpec(memory_space=pl.ANY)
 VMEM = pl.BlockSpec(memory_space=pltpu.VMEM)
+SMEM = pl.BlockSpec(memory_space=pltpu.SMEM)
 
 
 def call(kernel, rows, specs, *args, scratch=(), limit=24):
+    shapes = [jax.ShapeDtypeStruct((n, LANES), F32) for n in rows]
     return pl.pallas_call(
         kernel,
-        out_shape=jax.ShapeDtypeStruct((rows, LANES), F32),
+        out_shape=shapes,
         in_specs=specs,
-        out_specs=VMEM,
+        out_specs=[VMEM] * len(rows),
         scratch_shapes=scratch,
         compiler_params=pltpu.CompilerParams(vmem_limit_bytes=limit * 1024 * 1024),
     )(*args)
 
 
+def local_call(design, sign_bits, sampled, owner_map):
+    vmem, dma = pltpu.VMEM, pltpu.SemaphoreType.DMA
+    return call(
+        local_kernel,
+        [COLS * BLOCKS, TABLE],
+        [HBM] * 4,
+        design,
+        sign_bits.reshape(BLOCKS, LANES),
+        sampled.reshape(1, SAMPLED),
+        owner_map.reshape(1, SAMPLED),
+        scratch=[
+            vmem((ROWS, LANES), BF16),
+            vmem((BLOCKS, LANES), jnp.int32),
+            vmem((1, SAMPLED), jnp.int32),
+            vmem((1, SAMPLED), jnp.int32),
+            vmem((DEVICES, SAMPLED), F32),
+            vmem((DEVICES, SAMPLED), F32),
+            vmem((ROWS, LANES), F32),
+            vmem((ROWS, LANES), F32),
+            dma((PARTS,)),
+            dma((3,)),
+        ],
+    )
+
+
+def pick_call(me, columns, tables):
+    vmem, dma = pltpu.VMEM, pltpu.SemaphoreType.DMA
+    return call(
+        pick_kernel,
+        [DEVICES * CAP],
+        [SMEM, HBM, VMEM],
+        me,
+        columns,
+        tables,
+        scratch=[
+            vmem((DEVICES, BLOCKS, LANES), F32),
+            vmem((DEVICES * LISTED, LANES), F32),
+            vmem((DEVICES * CAP, LANES), F32),
+            dma((PARTS,)),
+        ],
+    )[0]
+
+
 def exchange(values):
     values = values.reshape(DEVICES, -1, LANES)
     return lax.all_to_all(values, AXES, split_axis=0, concat_axis=0, tiled=True)
 
 
 def gather_tables(table):
-    inner = lax.axis_size("inner")
-    near = [[g * 4 + i for i in range(4)] for g in range(inner // 4)]
-    far = [[g + 4 * i for i in range(inner // 4)] for g in range(4)]
-    table = lax.all_gather(table, "outer", axis=0, tiled=True)
-    table = lax.all_gather(table, "inner", axis=0, tiled=True, axis_index_groups=near)
-    return lax.all_gather(table, "inner", axis=0, tiled=True, axis_index_groups=far)
+    steps = (("outer", range(1, 4)), ("inner", range(1, 4)), ("inner", range(4, 32, 4)))
+    for axis, others in steps:
+        size = lax.axis_size(axis)
+        pieces = [
+            lax.ppermute(table, axis, [(place, place ^ other) for place in range(size)])
+            for other in others
+        ]
+        table = jnp.concatenate([table] + pieces, axis=0)
+    return table
 
 
 def per_device(design, sign_bits, sampled, owner_map):
-    vmem, dma = pltpu.VMEM, pltpu.SemaphoreType.DMA
-    table = call(
-        table_kernel,
-        TABLE,
-        [VMEM, VMEM],
-        sampled.reshape(1, SAMPLED),
-        owner_map.reshape(1, SAMPLED),
-        scratch=[vmem((DEVICES, SAMPLED), F32), vmem((DEVICES, SAMPLED), F32)],
-    )
+    me = lax.axis_index("inner") * lax.axis_size("outer") + lax.axis_index("outer")
+    columns, table = local_call(design, sign_bits, sampled, owner_map)
     tables = gather_tables(table)
-    columns = call(
-        local_kernel,
-        COLS * BLOCKS,
-        [HBM, HBM],
-        design,
-        sign_bits.reshape(BLOCKS, LANES),
-        scratch=[
-            vmem((ROWS, LANES), BF16),
-            vmem((BLOCKS, LANES), jnp.int32),
-            vmem((ROWS, LANES), F32),
-            vmem((ROWS, LANES), F32),
-            dma((PARTS,)),
-            dma(()),
-        ],
-    )
-    picked = call(
-        pick_kernel,
-        DEVICES * CAP,
-        [HBM, VMEM],
-        exchange(columns),
-        tables,
-        scratch=[
-            vmem((DEVICES, BLOCKS, LANES), F32),
-            vmem((8, LANES), F32),
-            vmem((DEVICES * CAP, LANES), F32),
-            dma((PARTS,)),
-        ],
-    )
-    tiles = call(turn_kernel, DEVICES * CAP, [VMEM], exchange(picked).reshape(-1, LANES))
+    picked = pick_call(me.astype(jnp.int32).reshape(1), exchange(columns), tables)
+    (tiles,) = call(turn_kernel, [DEVICES * CAP], [VMEM], exchange(picked).reshape(-1, LANES))
     return tiles.reshape(1, DEVICES, CAP, COLS)
 
 

time: 209 us -> 154 us (0.74)
  blocking collectives: 84.8 us -> 30.1 us
  starting transfers between devices: 12 us -> 31.5 us
  Pallas kernels: 40.4 us -> 26 us
  between operations: 13.5 us -> 0.14 us
  waiting for transfers between devices: 51.7 us -> 59.9 us
    ppermute x0 -> x13, waiting for transfers between devices: none -> 59.9 us  [gather_tables(): lax.ppermute(table, axis, [(place, place ^ other) for place in range(size)])]
    all_gather x2 -> x0, blocking collectives: 58.1 us -> none  [the longest x1 47.1 us: gather_tables(): table = lax.all_gather(table, 'outer', axis=0, tiled=True)]
    all_gather x1 -> x0, waiting for transfers between devices: 51.7 us -> none  [gather_tables(): lax.all_gather(table, 'inner', axis=0, tiled=True, axis_index_groups=far)]
    ppermute x0 -> x13, starting transfers between devices: none -> 19.5 us  [gather_tables(): lax.ppermute(table, axis, [(place, place ^ other) for place in range(size)])]
    pallas_call x4 -> x3, Pallas kernels: 40.4 us -> 26 us  [call(): pl.pallas_call(kernel, out_shape=shapes, in_specs=specs, out_specs=[VMEM]...]
    all_to_all x1, blocking collectives: 26.7 us -> 30.1 us  [exchange(): return lax.all_to_all(values, AXES, split_axis=0, concat_axis=0, tiled=True)]
    unnamed x12 -> x22, local copies, waits for them, and re-layouts: 5.73 us -> 5.85 us
  transfers between devices with their start and end apart: 2 -> 14, of which waited for: 1 -> 7; matrix products, arithmetic and copies ran while one was open for 0% -> 0% of each run, Pallas kernels for 0% -> 0%
where the time goes in v3:
time: 154 us
  waiting for transfers between devices  59.9 us (39%)
  starting transfers between devices  31.5 us (20%)
  blocking collectives  30.1 us (20%)
  Pallas kernels  26 us (17%)
  local copies, waits for them, and re-layouts  5.87 us (4%)
    ppermute x13, waiting for transfers between devices, gather_tables(): lax.ppermute(table, axis, [(place, place ^ other) for place in range(size)])  59.9 us
    all_to_all x1, blocking collectives, exchange(): return lax.all_to_all(values, AXES, split_axis=0, concat_axis=0, tiled=True)  30.1 us
    pallas_call x3, Pallas kernels, call(): pl.pallas_call(kernel, out_shape=shapes, in_specs=specs, out_specs=[VMEM]...  26 us
    ppermute x13, starting transfers between devices, gather_tables(): lax.ppermute(table, axis, [(place, place ^ other) for place in range(size)])  19.5 us
    all_to_all x1, starting transfers between devices, exchange(): return lax.all_to_all(values, AXES, split_axis=0, concat_axis=0, tiled=True)  12 us
    unnamed x22, local copies, waits for them, and re-layouts  5.85 us
  transfers between devices with their start and end apart: 14, of which 7 were waited for; matrix products, arithmetic and copies ran while one was open for 0% of the time, Pallas kernels for 0%

profile of v3, /device:TPU:1, one launch (start us, length us, event | category | flops | bytes accessed | tf_op | source)
XLA Modules:
  0.0 153.6 jit_solution(10444701776271156200)
XLA Ops:
  0.0 0.0 copy-start.1
  0.0 1.6 %copy-done.1 = bf16[8192,128]{1,0:T(8,128)(2,1)S(1)} copy-done((bf16[8192,128]{1,0:T(8,128)(2,1)S(1)}, bf16[8192,128]{1,0:T(8,128)(2,1)}, u32[]{:S(2)}) %copy-start.1) | copy-done | bytes 2097176
  1.6 0.0 copy-start.2
  1.6 0.8 copy-done.2
  2.4 0.0 copy-start.3
  2.4 0.7 copy-done.3
  3.0 0.0 copy-start.4
  3.0 0.7 copy-done.4
  3.7 8.7 %shard_map.46 = (f32[8192,128]{1,0:T(8,128)S(1)}, f32[24,128]{1,0:T(8,128)S(1)}) custom-call(bf16[8192,128]{1,0:T(8,128)(2,1)S(1)} %copy-done.1, s32[64,128]{1,0:T(8,128)S(1)} %bitcast.11, s32[1,1024]{1,0:T(1,128)S(1)} %bitcast.12, s32[1,1024]{1,0:T(1,128)S(1)} %bitcast.13), custom_call_target="tpu_custom_call" | custom-call | tf_op jit(solution)/shard_map/pallas_call | solution.py:256
  12.5 0.0 copy-start
  12.5 2.0 %copy-done = f32[8192,128]{1,0:T(8,128)} copy-done((f32[8192,128]{1,0:T(8,128)}, f32[8192,128]{1,0:T(8,128)S(1)}, u32[]{:S(2)}) %copy-start) | copy-done | bytes 4194328
  14.5 12.0 %all-to-all-start = ((f32[128,64,128]{2,1,0:T(8,128)}), f32[128,64,128]{2,1,0:T(8,128)}, u32[]{:S(2)}, u32[]{:S(2)}) async-start(f32[128,64,128]{2,1,0:T(8,128)} %bitcast.8), calls=%async_computation | async-start | bytes 8388608 | tf_op jit(solution)/shard_map/all_to_all | solution.py:311
  26.4 1.2 collective-permute-start
  27.7 0.6 collective-permute-start.1
  28.3 1.1 collective-permute-start.2
  29.4 0.0 collective-permute-done
  29.4 43.4 %collective-permute-done.1 = f32[24,128]{1,0:T(8,128)S(1)} collective-permute-done((f32[24,128]{1,0:T(8,128)S(1)}, f32[24,128]{1,0:T(8,128)S(1)}, u32[]{:S(2)}, u32[]{:S(2)}) %collective-permute-start.1) | collective-permute-done | bytes 12320 | tf_op jit(solution)/shard_map/ppermute | solution.py:319
  72.8 0.7 collective-permute-done.2
  73.6 1.3 collective-permute-start.3
  74.9 2.9 %collective-permute-start.4 = (f32[96,128]{1,0:T(8,128)S(1)}, f32[96,128]{1,0:T(8,128)S(1)}, u32[]{:S(2)}, u32[]{:S(2)}) collective-permute-start(f32[96,128]{1,0:T(8,128)S(1)} %get-tuple-element.17), channel_id=1, source_target_pairs={{0,8},{4,12},{8,0},{12,4},{16,24},{20,28},{24,16},{28,20},{32,40},... | collective-permute-start | bytes 147464 | tf_op jit(solution)/shard_map/ppermute | solution.py:319
  77.8 0.0 collective-permute-start.5
  77.8 0.6 collective-permute-done.3
  78.4 2.5 %collective-permute-done.4 = f32[96,128]{1,0:T(8,128)S(1)} collective-permute-done((f32[96,128]{1,0:T(8,128)S(1)}, f32[96,128]{1,0:T(8,128)S(1)}, u32[]{:S(2)}, u32[]{:S(2)}) %collective-permute-start.4) | collective-permute-done | bytes 49184 | tf_op jit(solution)/shard_map/ppermute | solution.py:319
  81.0 0.9 collective-permute-done.5
  81.9 2.5 %collective-permute-start.6 = (f32[384,128]{1,0:T(8,128)S(1)}, f32[384,128]{1,0:T(8,128)S(1)}, u32[]{:S(2)}, u32[]{:S(2)}) collective-permute-start(f32[384,128]{1,0:T(8,128)S(1)} %get-tuple-element.9), channel_id=1, source_target_pairs={{0,16},{4,20},{8,24},{12,28},{16,0},{20,4},{24,8},{28,12},{32,48},... | collective-permute-start | bytes 589832 | tf_op jit(solution)/shard_map/ppermute | solution.py:319
  84.5 1.2 collective-permute-start.7
  85.7 0.5 collective-permute-start.8
  86.2 2.8 %collective-permute-start.9 = (f32[384,128]{1,0:T(8,128)S(1)}, f32[384,128]{1,0:T(8,128)S(1)}, u32[]{:S(2)}, u32[]{:S(2)}) collective-permute-start(f32[384,128]{1,0:T(8,128)S(1)} %get-tuple-element.9), channel_id=1, source_target_pairs={{0,64},{4,68},{8,72},{12,76},{16,80},{20,84},{24,88},{28,92},{32,9... | collective-permute-start | bytes 589832 | tf_op jit(solution)/shard_map/ppermute | solution.py:319
  89.0 2.3 %collective-permute-start.10 = (f32[384,128]{1,0:T(8,128)S(1)}, f32[384,128]{1,0:T(8,128)S(1)}, u32[]{:S(2)}, u32[]{:S(2)}) collective-permute-start(f32[384,128]{1,0:T(8,128)S(1)} %get-tuple-element.9), channel_id=1, source_target_pairs={{0,80},{4,84},{8,88},{12,92},{16,64},{20,68},{24,72},{28,76},{32,1... | collective-permute-start | bytes 589832 | tf_op jit(solution)/shard_map/ppermute | solution.py:319
  91.3 0.0 collective-permute-done.6
  91.3 2.4 %collective-permute-start.11 = (f32[384,128]{1,0:T(8,128)S(1)}, f32[384,128]{1,0:T(8,128)S(1)}, u32[]{:S(2)}, u32[]{:S(2)}) collective-permute-start(f32[384,128]{1,0:T(8,128)S(1)} %get-tuple-element.9), channel_id=1, source_target_pairs={{0,96},{4,100},{8,104},{12,108},{16,112},{20,116},{24,120},{28,124... | collective-permute-start | bytes 589832 | tf_op jit(solution)/shard_map/ppermute | solution.py:319
  93.7 0.0 collective-permute-done.7
  93.7 0.7 collective-permute-start.12
  94.4 0.0 collective-permute-done.8
  94.4 8.5 %collective-permute-done.9 = f32[384,128]{1,0:T(8,128)S(1)} collective-permute-done((f32[384,128]{1,0:T(8,128)S(1)}, f32[384,128]{1,0:T(8,128)S(1)}, u32[]{:S(2)}, u32[]{:S(2)}) %collective-permute-start.9) | collective-permute-done | bytes 196640 | tf_op jit(solution)/shard_map/ppermute | solution.py:319
  102.9 0.0 collective-permute-done.10
  102.9 3.1 %collective-permute-done.11 = f32[384,128]{1,0:T(8,128)S(1)} collective-permute-done((f32[384,128]{1,0:T(8,128)S(1)}, f32[384,128]{1,0:T(8,128)S(1)}, u32[]{:S(2)}, u32[]{:S(2)}) %collective-permute-start.11) | collective-permute-done | bytes 196640 | tf_op jit(solution)/shard_map/ppermute | solution.py:319
  106.1 0.0 collective-permute-done.12
  106.1 0.0 all-to-all-done.column_hbm
  106.1 16.0 %shard_map.47 = f32[2048,128]{1,0:T(8,128)S(1)} custom-call(s32[1]{0:T(128)} %bitcast.me_ref, f32[128,64,128]{2,1,0:T(8,128)} %all-to-all-done.column_hbm, f32[3072,128]{1,0:T(8,128)S(1)} %constant_dynamic-update-slice_fusion.11.table_ref), custom_call_target="tpu_custom_call" | custom-call | tf_op jit(solution)/shard_map/pallas_call | solution.py:256
  122.1 30.1 %all_to_all.10 = f32[128,16,128]{2,1,0:T(8,128)S(1)} all-to-all(f32[128,16,128]{2,1,0:T(8,128)S(1)} %bitcast.10), channel_id=1, replica_groups=mesh['inner'=32,'outer'=4] {'inner','outer'}, dimensions={0} | all-to-all | bytes 2097152 | tf_op jit(solution)/shard_map/all_to_all | solution.py:311
  152.2 1.3 shard_map.48
  (14 shorter events, 0.1 us)
Async XLA Ops:
  0.0 1.6 %copy-start.1 = (bf16[8192,128]{1,0:T(8,128)(2,1)S(1)}, bf16[8192,128]{1,0:T(8,128)(2,1)}, u32[]{:S(2)}) copy-start(bf16[8192,128]{1,0:T(8,128)(2,1)} %design_hbm.1) | copy-start | bytes 6291460
  1.6 0.8 copy-start.2
  2.4 0.7 copy-start.3
  3.0 0.7 copy-start.4
  12.5 2.0 %copy-start = (f32[8192,128]{1,0:T(8,128)}, f32[8192,128]{1,0:T(8,128)S(1)}, u32[]{:S(2)}) copy-start(f32[8192,128]{1,0:T(8,128)S(1)} %get-tuple-element.7) | copy-start | bytes 12582916
  14.5 91.6 %all-to-all-start = ((f32[128,64,128]{2,1,0:T(8,128)}), f32[128,64,128]{2,1,0:T(8,128)}, u32[]{:S(2)}, u32[]{:S(2)}) async-start(f32[128,64,128]{2,1,0:T(8,128)} %bitcast.8), calls=%async_computation | async-start | bytes 8388608 | tf_op jit(solution)/shard_map/all_to_all | solution.py:311
  26.4 3.0 %collective-permute-start = (f32[24,128]{1,0:T(8,128)S(1)}, f32[24,128]{1,0:T(8,128)S(1)}, u32[]{:S(2)}, u32[]{:S(2)}) collective-permute-start(f32[24,128]{1,0:T(8,128)S(1)} %get-tuple-element.8), channel_id=1, source_target_pairs={{0,1},{1,0},{2,3},{3,2},{4,5},{5,4},{6,7},{7,6},{8,9},{9,8},{10,11... | collective-permute-start | bytes 36872 | tf_op jit(solution)/shard_map/ppermute | solution.py:319
  27.7 45.2 %collective-permute-start.1 = (f32[24,128]{1,0:T(8,128)S(1)}, f32[24,128]{1,0:T(8,128)S(1)}, u32[]{:S(2)}, u32[]{:S(2)}) collective-permute-start(f32[24,128]{1,0:T(8,128)S(1)} %get-tuple-element.8), channel_id=1, source_target_pairs={{0,2},{1,3},{2,0},{3,1},{4,6},{5,7},{6,4},{7,5},{8,10},{9,11},{10,... | collective-permute-start | bytes 36872 | tf_op jit(solution)/shard_map/ppermute | solution.py:319
  28.3 45.3 %collective-permute-start.2 = (f32[24,128]{1,0:T(8,128)S(1)}, f32[24,128]{1,0:T(8,128)S(1)}, u32[]{:S(2)}, u32[]{:S(2)}) collective-permute-start(f32[24,128]{1,0:T(8,128)S(1)} %get-tuple-element.8), channel_id=1, source_target_pairs={{0,3},{1,2},{2,1},{3,0},{4,7},{5,6},{6,5},{7,4},{8,11},{9,10},{10,... | collective-permute-start | bytes 36872 | tf_op jit(solution)/shard_map/ppermute | solution.py:319
  73.6 4.9 %collective-permute-start.3 = (f32[96,128]{1,0:T(8,128)S(1)}, f32[96,128]{1,0:T(8,128)S(1)}, u32[]{:S(2)}, u32[]{:S(2)}) collective-permute-start(f32[96,128]{1,0:T(8,128)S(1)} %get-tuple-element.17), channel_id=1, source_target_pairs={{0,4},{4,0},{8,12},{12,8},{16,20},{20,16},{24,28},{28,24},{32,36},... | collective-permute-start | bytes 147464 | tf_op jit(solution)/shard_map/ppermute | solution.py:319
  74.9 6.1 %collective-permute-start.4 = (f32[96,128]{1,0:T(8,128)S(1)}, f32[96,128]{1,0:T(8,128)S(1)}, u32[]{:S(2)}, u32[]{:S(2)}) collective-permute-start(f32[96,128]{1,0:T(8,128)S(1)} %get-tuple-element.17), channel_id=1, source_target_pairs={{0,8},{4,12},{8,0},{12,4},{16,24},{20,28},{24,16},{28,20},{32,40},... | collective-permute-start | bytes 147464 | tf_op jit(solution)/shard_map/ppermute | solution.py:319
  77.8 4.2 %collective-permute-start.5 = (f32[96,128]{1,0:T(8,128)S(1)}, f32[96,128]{1,0:T(8,128)S(1)}, u32[]{:S(2)}, u32[]{:S(2)}) collective-permute-start(f32[96,128]{1,0:T(8,128)S(1)} %get-tuple-element.17), channel_id=1, source_target_pairs={{0,12},{4,8},{8,4},{12,0},{16,28},{20,24},{24,20},{28,16},{32,44},... | collective-permute-start | bytes 147464 | tf_op jit(solution)/shard_map/ppermute | solution.py:319
  81.9 9.4 %collective-permute-start.6 = (f32[384,128]{1,0:T(8,128)S(1)}, f32[384,128]{1,0:T(8,128)S(1)}, u32[]{:S(2)}, u32[]{:S(2)}) collective-permute-start(f32[384,128]{1,0:T(8,128)S(1)} %get-tuple-element.9), channel_id=1, source_target_pairs={{0,16},{4,20},{8,24},{12,28},{16,0},{20,4},{24,8},{28,12},{32,48},... | collective-permute-start | bytes 589832 | tf_op jit(solution)/shard_map/ppermute | solution.py:319
  84.5 9.2 %collective-permute-start.7 = (f32[384,128]{1,0:T(8,128)S(1)}, f32[384,128]{1,0:T(8,128)S(1)}, u32[]{:S(2)}, u32[]{:S(2)}) collective-permute-start(f32[384,128]{1,0:T(8,128)S(1)} %get-tuple-element.9), channel_id=1, source_target_pairs={{0,32},{4,36},{8,40},{12,44},{16,48},{20,52},{24,56},{28,60},{32,0... | collective-permute-start | bytes 589832 | tf_op jit(solution)/shard_map/ppermute | solution.py:319
  85.7 8.7 %collective-permute-start.8 = (f32[384,128]{1,0:T(8,128)S(1)}, f32[384,128]{1,0:T(8,128)S(1)}, u32[]{:S(2)}, u32[]{:S(2)}) collective-permute-start(f32[384,128]{1,0:T(8,128)S(1)} %get-tuple-element.9), channel_id=1, source_target_pairs={{0,48},{4,52},{8,56},{12,60},{16,32},{20,36},{24,40},{28,44},{32,1... | collective-permute-start | bytes 589832 | tf_op jit(solution)/shard_map/ppermute | solution.py:319
  86.2 16.7 %collective-permute-start.9 = (f32[384,128]{1,0:T(8,128)S(1)}, f32[384,128]{1,0:T(8,128)S(1)}, u32[]{:S(2)}, u32[]{:S(2)}) collective-permute-start(f32[384,128]{1,0:T(8,128)S(1)} %get-tuple-element.9), channel_id=1, source_target_pairs={{0,64},{4,68},{8,72},{12,76},{16,80},{20,84},{24,88},{28,92},{32,9... | collective-permute-start | bytes 589832 | tf_op jit(solution)/shard_map/ppermute | solution.py:319
  89.0 13.9 %collective-permute-start.10 = (f32[384,128]{1,0:T(8,128)S(1)}, f32[384,128]{1,0:T(8,128)S(1)}, u32[]{:S(2)}, u32[]{:S(2)}) collective-permute-start(f32[384,128]{1,0:T(8,128)S(1)} %get-tuple-element.9), channel_id=1, source_target_pairs={{0,80},{4,84},{8,88},{12,92},{16,64},{20,68},{24,72},{28,76},{32,1... | collective-permute-start | bytes 589832 | tf_op jit(solution)/shard_map/ppermute | solution.py:319
  91.3 14.8 %collective-permute-start.11 = (f32[384,128]{1,0:T(8,128)S(1)}, f32[384,128]{1,0:T(8,128)S(1)}, u32[]{:S(2)}, u32[]{:S(2)}) collective-permute-start(f32[384,128]{1,0:T(8,128)S(1)} %get-tuple-element.9), channel_id=1, source_target_pairs={{0,96},{4,100},{8,104},{12,108},{16,112},{20,116},{24,120},{28,124... | collective-permute-start | bytes 589832 | tf_op jit(solution)/shard_map/ppermute | solution.py:319
  93.7 12.4 %collective-permute-start.12 = (f32[384,128]{1,0:T(8,128)S(1)}, f32[384,128]{1,0:T(8,128)S(1)}, u32[]{:S(2)}, u32[]{:S(2)}) collective-permute-start(f32[384,128]{1,0:T(8,128)S(1)} %get-tuple-element.9), channel_id=1, source_target_pairs={{0,112},{4,116},{8,120},{12,124},{16,96},{20,100},{24,104},{28,108... | collective-permute-start | bytes 589832 | tf_op jit(solution)/shard_map/ppermute | solution.py:319

commit v4 on v3

--- a/solution.py
+++ b/solution.py
@@ -16,7 +16,8 @@
 SAMPLED = 1024
 CAP = 16
 LISTED = SAMPLED // LANES
-TABLE = LISTED + CAP
+TABLE = 16
+DATA = BLOCKS + TABLE
 SCALE = 1.0 / math.sqrt(SAMPLED * DEVICES)
 PARTS = 8
 GROUP = 8
@@ -56,33 +57,44 @@
     return pl.ds(pl.multiple_of(start, 8), size)
 
 
-def slot_table(sampled, owners, at_slot, named):
+def slot_table(sampled, owners, at_row, named):
     one_hot = iota((DEVICES, SAMPLED), 0) == owners
+    one_hot16 = one_hot.astype(F32).astype(BF16)
     upto = iota((SAMPLED, SAMPLED), 0) <= iota((SAMPLED, SAMPLED), 1)
-    running = jnp.dot(
-        one_hot.astype(F32).astype(BF16), upto.astype(F32).astype(BF16), preferred_element_type=F32
-    )
-    position = jnp.sum(jnp.where(one_hot, running, 0.0), axis=0, keepdims=True) - 1.0
-    at_slot[...] = jnp.where(
-        iota((DEVICES, SAMPLED), 0) == position.astype(jnp.int32), 1.0, 0.0
-    )
-    place = iota((1, SAMPLED), 1) + 1
-    table = jnp.zeros((DEVICES, DEVICES), F32)
-    for part, weight in ((place >> 7, 128.0), (place & 127, 1.0)):
-        named[...] = jnp.where(one_hot, part.astype(F32), 0.0)
+    running = jnp.dot(one_hot16, upto.astype(F32).astype(BF16), preferred_element_type=F32)
+    counts = jnp.broadcast_to(running[:, SAMPLED - 1 :], (DEVICES, LANES))
+    below = iota((DEVICES, DEVICES), 1) < iota((DEVICES, DEVICES), 0)
+    starts = jnp.dot(
+        below.astype(F32).astype(BF16), counts.astype(BF16), preferred_element_type=F32
+    )
+    place = jnp.sum(
+        jnp.where(one_hot, running + starts[:, :1], 0.0), axis=0, keepdims=True
+    ).astype(jnp.int32) - 1
+    at_row[...] = jnp.where(iota((DEVICES, SAMPLED), 0) == place >> 7, 1.0, 0.0)
+    at_lane = iota((DEVICES, SAMPLED), 0) == place & (LANES - 1)
+    table = jnp.zeros((DEVICES, LANES), F32)
+    for part, weight in ((sampled >> 7, 128.0), (sampled & 127, 1.0)):
+        named[...] = jnp.where(at_lane, part.astype(F32), 0.0)
         table = table + weight * lax.dot_general(
-            at_slot[...].astype(BF16),
+            at_row[...].astype(BF16),
             named[...].astype(BF16),
             (((1,), (1,)), ((), ())),
             preferred_element_type=F32,
         )
-    listed = [sampled[:, row * LANES : (row + 1) * LANES].astype(F32) for row in range(LISTED)]
-    return jnp.concatenate(listed + [table[:CAP]], axis=0)
+    return jnp.concatenate(
+        [
+            table[:LISTED],
+            starts.T[:1],
+            counts.T[:1],
+            jnp.zeros((TABLE - LISTED - 2, LANES), F32),
+        ],
+        axis=0,
+    )
 
 
 def local_kernel(
-    design_hbm, signs_hbm, sampled_hbm, owner_hbm, out_ref, table_ref,
-    design, signs, sampled, owners, at_slot, named, mixed, turned, sems, small_sems,
+    design_hbm, signs_hbm, sampled_hbm, owner_hbm, out_ref,
+    design, signs, sampled, owners, at_row, named, mixed, turned, sems, small_sems,
 ):
     chunk = ROWS // PARTS
     small = [
@@ -104,7 +116,7 @@
     matrix = sylvester(order, order)
     for copy in small:
         copy.wait()
-    table_ref[...] = slot_table(sampled[...], owners[...], at_slot, named)
+    table = slot_table(sampled[...], owners[...], at_row, named)
     for n in range(PARTS):
         copies[n].wait()
         for pair in range(n * pairs // PARTS, (n + 1) * pairs // PARTS):
@@ -128,9 +140,10 @@
     @pl.loop(0, COLS, unroll=4)
     def _(column):
         for part in range(BLOCKS // 8):
-            out_ref[aligned(column * BLOCKS + part * 8, 8), :] = turned[
+            out_ref[aligned(column * DATA + part * 8, 8), :] = turned[
                 pl.ds(part * 8 * COLS + column, 8, stride=COLS), :
             ]
+        out_ref[aligned(column * DATA + BLOCKS, TABLE), :] = table
 
 
 def gather_rows(parts):
@@ -146,40 +159,31 @@
     return parts[0]
 
 
-def pick_kernel(me_ref, column_hbm, table_ref, out_ref, mixed, found, picked, sems):
-    me = me_ref[0]
-    copies = [
-        pltpu.make_async_copy(
-            column_hbm.at[:, pl.ds(8 * n, 8), :], mixed.at[:, pl.ds(8 * n, 8), :], sems.at[n]
-        )
-        for n in range(PARTS)
-    ]
-    for copy in copies:
-        copy.start()
-    for n in range(PARTS):
-        copies[n].wait()
-        rows = pl.ds(8 * n, 8)
-
-        @pl.loop(0, 8)
-        def _(low):
-            places = [high * 8 + low for high in range(16)]
-            values = butterflies([mixed[place, rows, :] for place in places])
-            for place, value in zip(places, values):
-                mixed[place, rows, :] = value
-
-        @pl.loop(0, 16)
-        def _(high):
-            places = [high * 8 + low for low in range(8)]
-            values = butterflies([mixed[place, rows, :] for place in places])
-            for place, value in zip(places, values):
-                mixed[place, rows, :] = value
+def pick_kernel(column_ref, out_ref, mixed, found, picked):
+    @pl.loop(0, BLOCKS)
+    def _(step):
+        part, low = step // 8, step % 8
+        places = [
+            aligned((high * 8 + low) * DATA + part * 8, 8) for high in range(16)
+        ]
+        values = butterflies([column_ref[place, :] for place in places])
+        for high, value in enumerate(values):
+            mixed[high * 8 + low, aligned(part * 8, 8), :] = value
+
+    @pl.loop(0, 2 * BLOCKS)
+    def _(step):
+        part, high = step // 16, step % 16
+        rows = aligned(part * 8, 8)
+        values = butterflies([mixed[high * 8 + low, rows, :] for low in range(8)])
+        for low, value in enumerate(values):
+            mixed[high * 8 + low, rows, :] = value
 
     place = iota((LANES, LANES), 0).astype(F32).astype(BF16)
     row8 = iota((8, LANES), 0)
     one, zero = jnp.ones((), BF16), jnp.zeros((), BF16)
 
     def pick(source):
-        listed = table_ref[aligned((source ^ me) * TABLE, LISTED), :].astype(jnp.int32)
+        listed = column_ref[aligned(source * DATA + BLOCKS, LISTED), :].astype(jnp.int32)
         key = (listed & (LANES - 1)).astype(F32)
         block = listed >> 7
         values = mixed[source]
@@ -205,10 +209,12 @@
         found[aligned(source * LISTED, LISTED), :] = gather_rows(parts)
 
     def place_in_slots(source):
-        slots = table_ref[aligned((source ^ me) * TABLE + LISTED, CAP), :].astype(jnp.int32) - 1
+        spans = column_ref[aligned(source * DATA + BLOCKS + LISTED, 8), :].astype(jnp.int32)
+        start, count = (jnp.broadcast_to(spans[n : n + 1], (8, LANES)) for n in range(2))
         here = found[aligned(source * LISTED, LISTED), :]
         for t in range(2):
-            slot = slots[8 * t : 8 * t + 8]
+            position = row8 + 8 * t
+            slot = start + position
             lane = slot & (LANES - 1)
             rows = [
                 jnp.take_along_axis(jnp.broadcast_to(here[r : r + 1], (8, LANES)), lane, axis=1)
@@ -218,7 +224,7 @@
                 odd = (slot >> (7 + n)) & 1 == 1
                 rows = [jnp.where(odd, b, a) for a, b in zip(rows[0::2], rows[1::2])]
             picked[aligned(source * CAP + 8 * t, 8), :] = jnp.where(
-                slot >= 0, rows[0] * SCALE, 0.0
+                position < count, rows[0] * SCALE, 0.0
             )
 
     for n in range(GROUP):
@@ -246,9 +252,8 @@
         ].T
 
 
-HBM = pl.BlockSpec(memory_space=pl.ANY)
+HBM = pl.BlockSpec(memory_space=pltpu.HBM)
 VMEM = pl.BlockSpec(memory_space=pltpu.VMEM)
-SMEM = pl.BlockSpec(memory_space=pltpu.SMEM)
 
 
 def call(kernel, rows, specs, *args, scratch=(), limit=24):
@@ -267,7 +272,7 @@
     vmem, dma = pltpu.VMEM, pltpu.SemaphoreType.DMA
     return call(
         local_kernel,
-        [COLS * BLOCKS, TABLE],
+        [COLS * DATA],
         [HBM] * 4,
         design,
         sign_bits.reshape(BLOCKS, LANES),
@@ -285,50 +290,34 @@
             dma((PARTS,)),
             dma((3,)),
         ],
-    )
-
-
-def pick_call(me, columns, tables):
-    vmem, dma = pltpu.VMEM, pltpu.SemaphoreType.DMA
+    )[0]
+
+
+def pick_call(columns):
     return call(
         pick_kernel,
         [DEVICES * CAP],
-        [SMEM, HBM, VMEM],
-        me,
+        [VMEM],
         columns,
-        tables,
         scratch=[
-            vmem((DEVICES, BLOCKS, LANES), F32),
-            vmem((DEVICES * LISTED, LANES), F32),
-            vmem((DEVICES * CAP, LANES), F32),
-            dma((PARTS,)),
+            pltpu.VMEM((DEVICES, BLOCKS, LANES), F32),
+            pltpu.VMEM((DEVICES * LISTED, LANES), F32),
+            pltpu.VMEM((DEVICES * CAP, LANES), F32),
         ],
     )[0]
 
 
 def exchange(values):
     values = values.reshape(DEVICES, -1, LANES)
-    return lax.all_to_all(values, AXES, split_axis=0, concat_axis=0, tiled=True)
-
-
-def gather_tables(table):
-    steps = (("outer", range(1, 4)), ("inner", range(1, 4)), ("inner", range(4, 32, 4)))
-    for axis, others in steps:
-        size = lax.axis_size(axis)
-        pieces = [
-            lax.ppermute(table, axis, [(place, place ^ other) for place in range(size)])
-            for other in others
-        ]
-        table = jnp.concatenate([table] + pieces, axis=0)
-    return table
+    return lax.all_to_all(values, AXES, split_axis=0, concat_axis=0, tiled=True).reshape(
+        -1, LANES
+    )
 
 
 def per_device(design, sign_bits, sampled, owner_map):
-    me = lax.axis_index("inner") * lax.axis_size("outer") + lax.axis_index("outer")
-    columns, table = local_call(design, sign_bits, sampled, owner_map)
-    tables = gather_tables(table)
-    picked = pick_call(me.astype(jnp.int32).reshape(1), exchange(columns), tables)
-    (tiles,) = call(turn_kernel, [DEVICES * CAP], [VMEM], exchange(picked).reshape(-1, LANES))
+    columns = exchange(local_call(design, sign_bits, sampled, owner_map))
+    picked = exchange(pick_call(columns))
+    (tiles,) = call(turn_kernel, [DEVICES * CAP], [VMEM], picked)
     return tiles.reshape(1, DEVICES, CAP, COLS)
 
 

time: 154 us -> 132 us (0.86)
  blocking collectives: 30.1 us -> 102 us
  waiting for transfers between devices: 59.9 us -> 0 us
  starting transfers between devices: 31.5 us -> 0 us
  local copies, waits for them, and re-layouts: 5.87 us -> 3.72 us
    all_to_all x1 -> x2, blocking collectives: 30.1 us -> 102 us  [exchange(): lax.all_to_all(values, AXES, split_axis=0, concat_axis=0, tiled=True)]
    ppermute x13 -> x0, waiting for transfers between devices: 59.9 us -> none  [gather_tables(): lax.ppermute(table, axis, [(place, place ^ other) for place in range(size)])]
    ppermute x13 -> x0, starting transfers between devices: 19.5 us -> none  [gather_tables(): lax.ppermute(table, axis, [(place, place ^ other) for place in range(size)])]
    all_to_all x1 -> x0, starting transfers between devices: 12 us -> none  [exchange(): return lax.all_to_all(values, AXES, split_axis=0, concat_axis=0, tiled=True)]
    unnamed x22 -> x8, local copies, waits for them, and re-layouts: 5.85 us -> 3.72 us
  transfers between devices with their start and end apart: 14 -> 0, of which waited for: 7 -> 0; matrix products, arithmetic and copies ran while one was open for 0% -> 0% of each run, Pallas kernels for 0% -> 0%
where the time goes in v4:
time: 132 us
  blocking collectives  102 us (77%)
  Pallas kernels  26.5 us (20%)
  local copies, waits for them, and re-layouts  3.72 us (3%)
    all_to_all x2, blocking collectives, exchange(): lax.all_to_all(values, AXES, split_axis=0, concat_axis=0, tiled=True)  102 us
    pallas_call x3, Pallas kernels, call(): pl.pallas_call(kernel, out_shape=shapes, in_specs=specs, out_specs=[VMEM]...  26.5 us
    unnamed x8, local copies, waits for them, and re-layouts  3.72 us

profile of v4, /device:TPU:1, one launch (start us, length us, event | category | flops | bytes accessed | tf_op | source)
XLA Modules:
  0.0 132.2 jit_solution(5506101718021516063)
XLA Ops:
  0.0 0.0 copy-start
  0.0 1.6 %copy-done = bf16[8192,128]{1,0:T(8,128)(2,1)S(1)} copy-done((bf16[8192,128]{1,0:T(8,128)(2,1)S(1)}, bf16[8192,128]{1,0:T(8,128)(2,1)}, u32[]{:S(2)}) %copy-start) | copy-done | bytes 2097176
  1.6 0.0 copy-start.1
  1.6 0.8 copy-done.1
  2.4 0.0 copy-start.2
  2.4 0.7 copy-done.2
  3.0 0.0 copy-start.3
  3.0 0.7 copy-done.3
  3.7 9.2 %shard_map.46 = f32[10240,128]{1,0:T(8,128)S(1)} custom-call(bf16[8192,128]{1,0:T(8,128)(2,1)S(1)} %copy-done, s32[64,128]{1,0:T(8,128)S(1)} %bitcast.12, s32[1,1024]{1,0:T(1,128)S(1)} %bitcast.13, s32[1,1024]{1,0:T(1,128)S(1)} %bitcast.14), custom_call_target="tpu_custom_call" | custom-call | tf_op jit(solution)/shard_map/pallas_call | solution.py:261
  13.0 75.7 %all_to_all.10 = f32[128,80,128]{2,1,0:T(8,128)S(1)} all-to-all(f32[128,80,128]{2,1,0:T(8,128)S(1)} %bitcast.9), channel_id=1, replica_groups=mesh['inner'=32,'outer'=4] {'inner','outer'}, dimensions={0} | all-to-all | bytes 10485760 | tf_op jit(solution)/shard_map/all_to_all | solution.py:312
  88.7 15.9 %shard_map.47 = f32[2048,128]{1,0:T(8,128)S(1)} custom-call(f32[10240,128]{1,0:T(8,128)S(1)} %bitcast.8), custom_call_target="tpu_custom_call" | custom-call | tf_op jit(solution)/shard_map/pallas_call | solution.py:261
  104.6 26.3 %all_to_all.11 = f32[128,16,128]{2,1,0:T(8,128)S(1)} all-to-all(f32[128,16,128]{2,1,0:T(8,128)S(1)} %bitcast.11), channel_id=1, replica_groups=mesh['inner'=32,'outer'=4] {'inner','outer'}, dimensions={0} | all-to-all | bytes 2097152 | tf_op jit(solution)/shard_map/all_to_all | solution.py:312
  130.8 1.3 %shard_map.48 = f32[2048,128]{1,0:T(8,128)} custom-call(f32[2048,128]{1,0:T(8,128)S(1)} %bitcast.10), custom_call_target="tpu_custom_call" | custom-call | tf_op jit(solution)/shard_map/pallas_call | solution.py:261
Async XLA Ops:
  0.0 1.6 %copy-start = (bf16[8192,128]{1,0:T(8,128)(2,1)S(1)}, bf16[8192,128]{1,0:T(8,128)(2,1)}, u32[]{:S(2)}) copy-start(bf16[8192,128]{1,0:T(8,128)(2,1)} %design_hbm.1) | copy-start | bytes 6291460
  1.6 0.8 copy-start.1
  2.4 0.7 copy-start.2
  3.0 0.7 copy-start.3

commit v5 on v4

--- a/solution.py
+++ b/solution.py
@@ -16,11 +16,12 @@
 SAMPLED = 1024
 CAP = 16
 LISTED = SAMPLED // LANES
-TABLE = 16
+TABLE = 8
 DATA = BLOCKS + TABLE
 SCALE = 1.0 / math.sqrt(SAMPLED * DEVICES)
 PARTS = 8
-GROUP = 8
+GROUP = 16
+BY_LANES = 5
 F32 = jnp.float32
 BF16 = jnp.bfloat16
 
@@ -81,15 +82,12 @@
             (((1,), (1,)), ((), ())),
             preferred_element_type=F32,
         )
-    return jnp.concatenate(
-        [
-            table[:LISTED],
-            starts.T[:1],
-            counts.T[:1],
-            jnp.zeros((TABLE - LISTED - 2, LANES), F32),
-        ],
-        axis=0,
-    )
+    half = LISTED // 2
+    rest = [starts.T[:1], counts.T[:1], jnp.zeros((TABLE - half - 2, LANES), F32)]
+    return [
+        jnp.concatenate([table[:half]] + rest, axis=0),
+        jnp.concatenate([table[half:LISTED]] + rest, axis=0),
+    ]
 
 
 def local_kernel(
@@ -116,7 +114,7 @@
     matrix = sylvester(order, order)
     for copy in small:
         copy.wait()
-    table = slot_table(sampled[...], owners[...], at_row, named)
+    halves = slot_table(sampled[...], owners[...], at_row, named)
     for n in range(PARTS):
         copies[n].wait()
         for pair in range(n * pairs // PARTS, (n + 1) * pairs // PARTS):
@@ -137,13 +135,15 @@
         rows = slice(block * LANES, (block + 1) * LANES)
         turned[rows, :] = mixed[rows, :].T
 
-    @pl.loop(0, COLS, unroll=4)
-    def _(column):
-        for part in range(BLOCKS // 8):
-            out_ref[aligned(column * DATA + part * 8, 8), :] = turned[
-                pl.ds(part * 8 * COLS + column, 8, stride=COLS), :
-            ]
-        out_ref[aligned(column * DATA + BLOCKS, TABLE), :] = table
+    @pl.loop(0, COLS // 2, unroll=2)
+    def _(pair):
+        for t in range(2):
+            column = 2 * pair + t
+            for part in range(BLOCKS // 8):
+                out_ref[aligned(column * DATA + part * 8, 8), :] = turned[
+                    pl.ds(part * 8 * COLS + column, 8, stride=COLS), :
+                ]
+            out_ref[aligned(column * DATA + BLOCKS, TABLE), :] = halves[t]
 
 
 def gather_rows(parts):
@@ -159,34 +159,57 @@
     return parts[0]
 
 
-def pick_kernel(column_ref, out_ref, mixed, found, picked):
-    @pl.loop(0, BLOCKS)
+def mix_kernel(column_ref, out_ref):
+    @pl.loop(0, BLOCKS, unroll=4)
     def _(step):
         part, low = step // 8, step % 8
-        places = [
-            aligned((high * 8 + low) * DATA + part * 8, 8) for high in range(16)
-        ]
-        values = butterflies([column_ref[place, :] for place in places])
-        for high, value in enumerate(values):
-            mixed[high * 8 + low, aligned(part * 8, 8), :] = value
-
-    @pl.loop(0, 2 * BLOCKS)
+        places = [high * 8 + low for high in range(16)]
+        values = butterflies(
+            [column_ref[aligned(place * DATA + part * 8, 8), :] for place in places]
+        )
+        for place, value in zip(places, values):
+            out_ref[aligned(place * BLOCKS + part * 8, 8), :] = value
+
+    @pl.loop(0, 2 * BLOCKS, unroll=4)
     def _(step):
         part, high = step // 16, step % 16
-        rows = aligned(part * 8, 8)
-        values = butterflies([mixed[high * 8 + low, rows, :] for low in range(8)])
-        for low, value in enumerate(values):
-            mixed[high * 8 + low, rows, :] = value
-
+        transform_in_place(
+            out_ref,
+            [aligned((high * 8 + low) * BLOCKS + part * 8, 8) for low in range(8)],
+        )
+
+
+def pick_kernel(core_ref, mixed, own_ref, other_ref, out_ref, found, picked):
+    first = core_ref[0] == 0
     place = iota((LANES, LANES), 0).astype(F32).astype(BF16)
     row8 = iota((8, LANES), 0)
     one, zero = jnp.ones((), BF16), jnp.zeros((), BF16)
 
-    def pick(source):
-        listed = column_ref[aligned(source * DATA + BLOCKS, LISTED), :].astype(jnp.int32)
+    def samples(source):
+        rows = aligned(source * TABLE, TABLE)
+        own, other = own_ref[rows, :], other_ref[rows, :]
+        lower, upper = jnp.where(first, own, other), jnp.where(first, other, own)
+        half = LISTED // 2
+        return jnp.concatenate([lower[:half], upper[:half]], axis=0).astype(jnp.int32)
+
+    def pick_by_lanes(source):
+        listed = samples(source)
+        lane, block = listed & (LANES - 1), listed >> 7
+
+        def choose(low, level):
+            if level == 0:
+                row = mixed[pl.ds(source * BLOCKS + low, 1), :]
+                return jnp.take_along_axis(jnp.broadcast_to(row, (8, LANES)), lane, axis=1)
+            a, b = choose(low, level - 1), choose(low + (1 << (level - 1)), level - 1)
+            return jnp.where((block >> (level - 1)) & 1 == 1, b, a)
+
+        found[aligned(source * LISTED, LISTED), :] = choose(0, 6)
+
+    def pick_by_matmul(source):
+        listed = samples(source)
         key = (listed & (LANES - 1)).astype(F32)
         block = listed >> 7
-        values = mixed[source]
+        values = mixed[aligned(source * BLOCKS, BLOCKS), :]
         top = values.astype(BF16)
         operand = jnp.concatenate([top, (values - top.astype(F32)).astype(BF16)], axis=0)
         parts = []
@@ -208,9 +231,13 @@
             parts.append(jnp.where(wanted & 7 == row8, values[0], 0.0))
         found[aligned(source * LISTED, LISTED), :] = gather_rows(parts)
 
+    def pick(group, n):
+        every = GROUP // BY_LANES if BY_LANES else GROUP + 1
+        (pick_by_lanes if (n + 1) % every == 0 else pick_by_matmul)(group * GROUP + n)
+
     def place_in_slots(source):
-        spans = column_ref[aligned(source * DATA + BLOCKS + LISTED, 8), :].astype(jnp.int32)
-        start, count = (jnp.broadcast_to(spans[n : n + 1], (8, LANES)) for n in range(2))
+        spans = own_ref[aligned(source * TABLE, TABLE), :].astype(jnp.int32)
+        start, count = (jnp.broadcast_to(spans[n : n + 1], (8, LANES)) for n in (4, 5))
         here = found[aligned(source * LISTED, LISTED), :]
         for t in range(2):
             position = row8 + 8 * t
@@ -228,13 +255,13 @@
             )
 
     for n in range(GROUP):
-        pick(n)
+        pick(0, n)
 
     @pl.loop(1, DEVICES // GROUP)
     def _(group):
         for n in range(GROUP):
             place_in_slots((group - 1) * GROUP + n)
-            pick(group * GROUP + n)
+            pick(group, n)
 
     for n in range(GROUP):
         place_in_slots(DEVICES - GROUP + n)
@@ -254,6 +281,7 @@
 
 HBM = pl.BlockSpec(memory_space=pltpu.HBM)
 VMEM = pl.BlockSpec(memory_space=pltpu.VMEM)
+SMEM = pl.BlockSpec(memory_space=pltpu.SMEM)
 
 
 def call(kernel, rows, specs, *args, scratch=(), limit=24):
@@ -293,14 +321,20 @@
     )[0]
 
 
-def pick_call(columns):
+def mix_call(columns):
+    return call(mix_kernel, [DEVICES * BLOCKS], [VMEM], columns)[0]
+
+
+def pick_call(core, mixed, own, other):
     return call(
         pick_kernel,
         [DEVICES * CAP],
-        [VMEM],
-        columns,
+        [SMEM, VMEM, VMEM, VMEM],
+        core,
+        mixed,
+        own,
+        other,
         scratch=[
-            pltpu.VMEM((DEVICES, BLOCKS, LANES), F32),
             pltpu.VMEM((DEVICES * LISTED, LANES), F32),
             pltpu.VMEM((DEVICES * CAP, LANES), F32),
         ],
@@ -308,7 +342,7 @@
 
 
 def exchange(values):
-    values = values.reshape(DEVICES, -1, LANES)
+    values = values.reshape(DEVICES, 1, -1)
     return lax.all_to_all(values, AXES, split_axis=0, concat_axis=0, tiled=True).reshape(
         -1, LANES
     )
@@ -316,7 +350,11 @@
 
 def per_device(design, sign_bits, sampled, owner_map):
     columns = exchange(local_call(design, sign_bits, sampled, owner_map))
-    picked = exchange(pick_call(columns))
+    own = columns.reshape(DEVICES, DATA, LANES)[:, BLOCKS:].reshape(-1, LANES)
+    cores = [(place, place ^ 1) for place in range(lax.axis_size("outer"))]
+    other = lax.ppermute(own, "outer", cores)
+    core = (lax.axis_index("outer") & 1).astype(jnp.int32).reshape(1)
+    picked = exchange(pick_call(core, mix_call(columns), own, other))
     (tiles,) = call(turn_kernel, [DEVICES * CAP], [VMEM], picked)
     return tiles.reshape(1, DEVICES, CAP, COLS)
 

time: 132 us -> 127 us (0.962)
  blocking collectives: 102 us -> 96.4 us
  Pallas kernels: 26.5 us -> 21.5 us
  local copies, waits for them, and re-layouts: 3.72 us -> 8.21 us
    all_to_all x2, blocking collectives: 102 us -> 96.4 us  [exchange(): lax.all_to_all(values, AXES, split_axis=0, concat_axis=0, tiled=True)]
    pallas_call x3 -> x4, Pallas kernels: 26.5 us -> 21.5 us  [call(): pl.pallas_call(kernel, out_shape=shapes, in_specs=specs, out_specs=[VMEM]...]
    unnamed x8 -> x12, local copies, waits for them, and re-layouts: 3.72 us -> 8.18 us
  transfers between devices with their start and end apart: 0 -> 1, of which waited for: 0 -> 0; matrix products, arithmetic and copies ran while one was open for 0% -> 0% of each run, Pallas kernels for 0% -> 2%
where the time goes in v5:
time: 127 us
  blocking collectives  96.4 us (76%)
  Pallas kernels  21.5 us (17%)
  local copies, waits for them, and re-layouts  8.21 us (6%)
    all_to_all x2, blocking collectives, exchange(): lax.all_to_all(values, AXES, split_axis=0, concat_axis=0, tiled=True)  96.4 us
    pallas_call x4, Pallas kernels, call(): pl.pallas_call(kernel, out_shape=shapes, in_specs=specs, out_specs=[VMEM]...  21.5 us
    unnamed x12, local copies, waits for them, and re-layouts  8.18 us
  transfers between devices with their start and end apart: 1, of which 0 were waited for; matrix products, arithmetic and copies ran while one was open for 0% of the time, Pallas kernels for 2%

profile of v5, /device:TPU:1, one launch (start us, length us, event | category | flops | bytes accessed | tf_op | source)
XLA Modules:
  0.0 126.6 jit_solution(12467011119773841335)
XLA Ops:
  0.0 0.0 copy-start.2
  0.0 1.6 %copy-done.2 = bf16[8192,128]{1,0:T(8,128)(2,1)S(1)} copy-done((bf16[8192,128]{1,0:T(8,128)(2,1)S(1)}, bf16[8192,128]{1,0:T(8,128)(2,1)}, u32[]{:S(2)}) %copy-start.2) | copy-done | bytes 2097176
  1.6 0.0 copy-start.3
  1.6 0.8 copy-done.3
  2.4 0.0 copy-start.4
  2.4 0.7 copy-done.4
  3.0 0.0 copy-start.5
  3.0 0.7 copy-done.5
  3.7 9.2 %shard_map.46 = f32[9216,128]{1,0:T(8,128)S(1)} custom-call(bf16[8192,128]{1,0:T(8,128)(2,1)S(1)} %copy-done.2, s32[64,128]{1,0:T(8,128)S(1)} %bitcast.17, s32[1,1024]{1,0:T(1,128)S(1)} %bitcast.18, s32[1,1024]{1,0:T(1,128)S(1)} %bitcast.19), custom_call_target="tpu_custom_call" | custom-call | tf_op jit(solution)/shard_map/pallas_call | solution.py:289
  12.9 70.4 %all_to_all.10 = f32[128,1,9216]{2,1,0:T(1,128)S(1)} all-to-all(f32[128,1,9216]{2,1,0:T(1,128)S(1)} %bitcast.14), channel_id=1, replica_groups=mesh['inner'=32,'outer'=4] {'inner','outer'}, dimensions={0} | all-to-all | bytes 9437184 | tf_op jit(solution)/shard_map/all_to_all | solution.py:346
  83.4 0.0 copy-start
  83.4 2.1 %copy-done = f32[128,1,9216]{2,1,0:T(1,128)} copy-done((f32[128,1,9216]{2,1,0:T(1,128)}, f32[128,1,9216]{2,1,0:T(1,128)S(1)}, u32[]{:S(2)}) %copy-start) | copy-done | bytes 4718616
  85.6 0.4 collective-permute-start
  86.0 0.0 copy-start.1
  86.0 2.3 %copy-done.1 = f32[128,1,9216]{2,1,0:T(1,128)S(1)} copy-done((f32[128,1,9216]{2,1,0:T(1,128)S(1)}, f32[128,1,9216]{2,1,0:T(1,128)}, u32[]{:S(2)}) %copy-start.1) | copy-done | bytes 4718616
  88.3 2.5 %shard_map.47.mixed = f32[8192,128]{1,0:T(8,128)S(1)} custom-call(f32[9216,128]{1,0:T(8,128)S(1)} %bitcast.13), custom_call_target="tpu_custom_call" | custom-call | tf_op jit(solution)/shard_map/pallas_call | solution.py:289
  90.8 0.0 collective-permute-done.other_ref
  90.8 8.5 %shard_map.48 = f32[2048,128]{1,0:T(8,128)S(1)} custom-call(s32[1]{0:T(128)} %bitcast.core_ref, f32[8192,128]{1,0:T(8,128)S(1)} %shard_map.47.mixed, f32[1024,128]{1,0:T(8,128)S(1)} %slice_bitcast_fusion.own_ref, f32[1024,128]{1,0:T(8,128)S(1)} %collective-permute-done.other_ref), custom_call_target="tpu_custom_call" | custom-call | tf_op jit(solution)/shard_map/pallas_call | solution.py:289
  99.3 25.9 %all_to_all.11 = f32[128,1,2048]{2,1,0:T(1,128)S(1)} all-to-all(f32[128,1,2048]{2,1,0:T(1,128)S(1)} %bitcast.15), channel_id=1, replica_groups=mesh['inner'=32,'outer'=4] {'inner','outer'}, dimensions={0} | all-to-all | bytes 2097152 | tf_op jit(solution)/shard_map/all_to_all | solution.py:346
  125.2 1.3 %shard_map.49 = f32[2048,128]{1,0:T(8,128)} custom-call(f32[2048,128]{1,0:T(8,128)S(1)} %bitcast.16), custom_call_target="tpu_custom_call" | custom-call | tf_op jit(solution)/shard_map/pallas_call | solution.py:289
  (1 shorter events, 0.0 us)
Async XLA Ops:
  0.0 1.6 %copy-start.2 = (bf16[8192,128]{1,0:T(8,128)(2,1)S(1)}, bf16[8192,128]{1,0:T(8,128)(2,1)}, u32[]{:S(2)}) copy-start(bf16[8192,128]{1,0:T(8,128)(2,1)} %design_hbm.1) | copy-start | bytes 6291460
  1.6 0.8 copy-start.3
  2.4 0.7 copy-start.4
  3.0 0.7 copy-start.5
  83.4 2.1 %copy-start = (f32[128,1,9216]{2,1,0:T(1,128)}, f32[128,1,9216]{2,1,0:T(1,128)S(1)}, u32[]{:S(2)}) copy-start(f32[128,1,9216]{2,1,0:T(1,128)S(1)} %all_to_all.10) | copy-start | bytes 14155780
  85.6 5.3 %collective-permute-start = (f32[1024,128]{1,0:T(8,128)S(1)}, f32[1024,128]{1,0:T(8,128)S(1)}, u32[]{:S(2)}, u32[]{:S(2)}) collective-permute-start(f32[1024,128]{1,0:T(8,128)S(1)} %slice_bitcast_fusion.own_ref), channel_id=1, source_target_pairs={{0,1},{1,0},{2,3},{3,2},{4,5},{5,4},{6,7},{7,6},{8,9},{9,8},{10,11... | collective-permute-start | bytes 1572872 | tf_op jit(solution)/shard_map/ppermute | solution.py:355
  86.0 2.3 %copy-start.1 = (f32[128,1,9216]{2,1,0:T(1,128)S(1)}, f32[128,1,9216]{2,1,0:T(1,128)}, u32[]{:S(2)}) copy-start(f32[128,1,9216]{2,1,0:T(1,128)} %copy-done) | copy-start | bytes 14155780

commit v6 on v5

--- a/solution.py
+++ b/solution.py
@@ -74,7 +74,8 @@
     at_row[...] = jnp.where(iota((DEVICES, SAMPLED), 0) == place >> 7, 1.0, 0.0)
     at_lane = iota((DEVICES, SAMPLED), 0) == place & (LANES - 1)
     table = jnp.zeros((DEVICES, LANES), F32)
-    for part, weight in ((sampled >> 7, 128.0), (sampled & 127, 1.0)):
+    block = ((sampled >> 7 & 1) << 5) + (sampled >> 8)
+    for part, weight in ((block, 128.0), (sampled & 127, 1.0)):
         named[...] = jnp.where(at_lane, part.astype(F32), 0.0)
         table = table + weight * lax.dot_general(
             at_row[...].astype(BF16),
@@ -91,8 +92,8 @@
 
 
 def local_kernel(
-    design_hbm, signs_hbm, sampled_hbm, owner_hbm, out_ref,
-    design, signs, sampled, owners, at_row, named, mixed, turned, sems, small_sems,
+    design_hbm, signs_hbm, sampled_hbm, owner_hbm, out_hbm,
+    design, signs, sampled, owners, at_row, named, mixed, turned, out, sems, small_sems, out_sems,
 ):
     chunk = ROWS // PARTS
     small = [
@@ -131,19 +132,41 @@
             mixed, [aligned(pair * order + slab * 8, 8) for pair in range(pairs)]
         )
 
-    for block in range(BLOCKS):
-        rows = slice(block * LANES, (block + 1) * LANES)
-        turned[rows, :] = mixed[rows, :].T
-
-    @pl.loop(0, COLS // 2, unroll=2)
-    def _(pair):
-        for t in range(2):
-            column = 2 * pair + t
-            for part in range(BLOCKS // 8):
-                out_ref[aligned(column * DATA + part * 8, 8), :] = turned[
-                    pl.ds(part * 8 * COLS + column, 8, stride=COLS), :
-                ]
-            out_ref[aligned(column * DATA + BLOCKS, TABLE), :] = halves[t]
+    for t in range(2):
+        for pair in range(pairs):
+            place = t * pairs + pair
+            turned[place * LANES : (place + 1) * LANES, :] = mixed[
+                (2 * pair + t) * LANES : (2 * pair + t + 1) * LANES, :
+            ].T
+
+    columns = COLS // PARTS
+
+    def send(step):
+        rows = aligned(step * columns * DATA, columns * DATA)
+        return pltpu.make_async_copy(out.at[rows], out_hbm.at[rows], out_sems.at[step])
+
+    @pl.loop(0, PARTS)
+    def _(step):
+        for part in range(BLOCKS // 8):
+            for first in range(0, columns, 8):
+                tile = jnp.stack(
+                    [
+                        turned[aligned((part * 8 + n) * COLS + step * columns + first, 8), :]
+                        for n in range(8)
+                    ]
+                )
+                tile = jnp.swapaxes(tile, 0, 1)
+                for n in range(8):
+                    place = (step * columns + first + n) * DATA + part * 8
+                    out[aligned(place, 8), :] = tile[n]
+        for n in range(columns):
+            place = (step * columns + n) * DATA + BLOCKS
+            out[aligned(place, TABLE), :] = halves[n % 2]
+        send(step).start()
+
+    @pl.loop(0, PARTS)
+    def _(step):
+        send(step).wait()
 
 
 def gather_rows(parts):
@@ -179,8 +202,8 @@
         )
 
 
-def pick_kernel(core_ref, mixed, own_ref, other_ref, out_ref, found, picked):
-    first = core_ref[0] == 0
+def pick_kernel(mixed, own_ref, other_ref, out_ref, found, picked):
+    first = lax.axis_index("outer") % 2 == 0
     place = iota((LANES, LANES), 0).astype(F32).astype(BF16)
     row8 = iota((8, LANES), 0)
     one, zero = jnp.ones((), BF16), jnp.zeros((), BF16)
@@ -281,16 +304,15 @@
 
 HBM = pl.BlockSpec(memory_space=pltpu.HBM)
 VMEM = pl.BlockSpec(memory_space=pltpu.VMEM)
-SMEM = pl.BlockSpec(memory_space=pltpu.SMEM)
-
-
-def call(kernel, rows, specs, *args, scratch=(), limit=24):
+
+
+def call(kernel, rows, specs, *args, scratch=(), limit=24, out=VMEM):
     shapes = [jax.ShapeDtypeStruct((n, LANES), F32) for n in rows]
     return pl.pallas_call(
         kernel,
         out_shape=shapes,
         in_specs=specs,
-        out_specs=[VMEM] * len(rows),
+        out_specs=[out] * len(rows),
         scratch_shapes=scratch,
         compiler_params=pltpu.CompilerParams(vmem_limit_bytes=limit * 1024 * 1024),
     )(*args)
@@ -315,9 +337,13 @@
             vmem((DEVICES, SAMPLED), F32),
             vmem((ROWS, LANES), F32),
             vmem((ROWS, LANES), F32),
+            vmem((COLS * DATA, LANES), F32),
             dma((PARTS,)),
             dma((3,)),
+            dma((PARTS,)),
         ],
+        limit=60,
+        out=HBM,
     )[0]
 
 
@@ -325,12 +351,11 @@
     return call(mix_kernel, [DEVICES * BLOCKS], [VMEM], columns)[0]
 
 
-def pick_call(core, mixed, own, other):
+def pick_call(mixed, own, other):
     return call(
         pick_kernel,
         [DEVICES * CAP],
-        [SMEM, VMEM, VMEM, VMEM],
-        core,
+        [VMEM, VMEM, VMEM],
         mixed,
         own,
         other,
@@ -353,8 +378,7 @@
     own = columns.reshape(DEVICES, DATA, LANES)[:, BLOCKS:].reshape(-1, LANES)
     cores = [(place, place ^ 1) for place in range(lax.axis_size("outer"))]
     other = lax.ppermute(own, "outer", cores)
-    core = (lax.axis_index("outer") & 1).astype(jnp.int32).reshape(1)
-    picked = exchange(pick_call(core, mix_call(columns), own, other))
+    picked = exchange(pick_call(mix_call(columns), own, other))
     (tiles,) = call(turn_kernel, [DEVICES * CAP], [VMEM], picked)
     return tiles.reshape(1, DEVICES, CAP, COLS)
 

time: 127 us -> 119 us (0.937)
  local copies, waits for them, and re-layouts: 8.21 us -> 0.03 us
    unnamed x12 -> x0, local copies, waits for them, and re-layouts: 8.18 us -> none
where the time goes in v6:
time: 119 us
  blocking collectives  96.6 us (81%)
  Pallas kernels  21.9 us (18%)
    all_to_all x2, blocking collectives, exchange(): lax.all_to_all(values, AXES, split_axis=0, concat_axis=0, tiled=True)  96.6 us
    pallas_call x4, Pallas kernels, call(): pl.pallas_call(kernel, out_shape=shapes, in_specs=specs, out_specs=[out]...  21.9 us
  transfers between devices with their start and end apart: 1, of which 0 were waited for; matrix products, arithmetic and copies ran while one was open for 0% of the time, Pallas kernels for 2%

profile of v6, /device:TPU:1, one launch (start us, length us, event | category | flops | bytes accessed | tf_op | source)
XLA Modules:
  0.0 119.1 jit_solution(11463650870684189276)
XLA Ops:
  0.0 9.6 %shard_map.46 = f32[9216,128]{1,0:T(8,128)} custom-call(bf16[8192,128]{1,0:T(8,128)(2,1)} %design_hbm.1, s32[64,128]{1,0:T(8,128)} %bitcast.16, s32[1,1024]{1,0:T(1,128)} %bitcast.17, s32[1,1024]{1,0:T(1,128)} %bitcast.18), custom_call_target="tpu_custom_call" | custom-call | tf_op jit(solution)/shard_map/pallas_call | solution.py:311
  9.6 70.7 %all_to_all.10 = f32[128,1,9216]{2,1,0:T(1,128)S(1)} all-to-all(f32[128,1,9216]{2,1,0:T(1,128)} %bitcast.15), channel_id=1, replica_groups=mesh['inner'=32,'outer'=4] {'inner','outer'}, dimensions={0} | all-to-all | bytes 9437184 | tf_op jit(solution)/shard_map/all_to_all | solution.py:371
  80.3 0.5 collective-permute-start
  80.8 2.5 %shard_map.47.mixed = f32[8192,128]{1,0:T(8,128)S(1)} custom-call(f32[9216,128]{1,0:T(8,128)S(1)} %bitcast.12), custom_call_target="tpu_custom_call" | custom-call | tf_op jit(solution)/shard_map/pallas_call | solution.py:311
  83.4 0.0 collective-permute-done.other_ref
  83.4 8.4 %shard_map.48 = f32[2048,128]{1,0:T(8,128)S(1)} custom-call(f32[8192,128]{1,0:T(8,128)S(1)} %shard_map.47.mixed, f32[1024,128]{1,0:T(8,128)S(1)} %slice_bitcast_fusion.own_ref, f32[1024,128]{1,0:T(8,128)S(1)} %collective-permute-done.other_ref), custom_call_target="tpu_custom_call" | custom-call | tf_op jit(solution)/shard_map/pallas_call | solution.py:311
  91.8 25.9 %all_to_all.11 = f32[128,1,2048]{2,1,0:T(1,128)S(1)} all-to-all(f32[128,1,2048]{2,1,0:T(1,128)S(1)} %bitcast.14), channel_id=1, replica_groups=mesh['inner'=32,'outer'=4] {'inner','outer'}, dimensions={0} | all-to-all | bytes 2097152 | tf_op jit(solution)/shard_map/all_to_all | solution.py:371
  117.7 1.3 %shard_map.49 = f32[2048,128]{1,0:T(8,128)} custom-call(f32[2048,128]{1,0:T(8,128)S(1)} %bitcast.13), custom_call_target="tpu_custom_call" | custom-call | tf_op jit(solution)/shard_map/pallas_call | solution.py:311
  (1 shorter events, 0.0 us)
Async XLA Ops:
  80.3 3.0 %collective-permute-start = (f32[1024,128]{1,0:T(8,128)S(1)}, f32[1024,128]{1,0:T(8,128)S(1)}, u32[]{:S(2)}, u32[]{:S(2)}) collective-permute-start(f32[1024,128]{1,0:T(8,128)S(1)} %slice_bitcast_fusion.own_ref), channel_id=1, source_target_pairs={{0,1},{1,0},{2,3},{3,2},{4,5},{5,4},{6,7},{7,6},{8,9},{9,8},{10,11... | collective-permute-start | bytes 1572872 | tf_op jit(solution)/shard_map/ppermute | solution.py:380

commit v7 on v6

--- a/solution.py
+++ b/solution.py
@@ -7,7 +7,9 @@
 from jax.experimental.pallas import tpu as pltpu
 from jax.sharding import PartitionSpec as P
 
-AXES = ("inner", "outer")
+AXES = ("y", "h", "z", "l", "c")
+SIZES = (4, 2, 4, 2, 2)
+ORDER = ("y", "z", "h", "l", "c")
 DEVICES = 128
 COLS = 128
 LANES = 128
@@ -58,8 +60,16 @@
     return pl.ds(pl.multiple_of(start, 8), size)
 
 
+def rank_of(place):
+    return (place & 99) + ((place >> 2 & 3) << 3) + ((place >> 4 & 1) << 2)
+
+
+def place_of(rank):
+    return (rank & 99) + ((rank >> 3 & 3) << 2) + ((rank >> 2 & 1) << 4)
+
+
 def slot_table(sampled, owners, at_row, named):
-    one_hot = iota((DEVICES, SAMPLED), 0) == owners
+    one_hot = iota((DEVICES, SAMPLED), 0) == rank_of(owners)
     one_hot16 = one_hot.astype(F32).astype(BF16)
     upto = iota((SAMPLED, SAMPLED), 0) <= iota((SAMPLED, SAMPLED), 1)
     running = jnp.dot(one_hot16, upto.astype(F32).astype(BF16), preferred_element_type=F32)
@@ -126,7 +136,7 @@
             rows = pl.ds(pair * order, order)
             mixed[rows, :] = jnp.dot(signed, design[rows, :], preferred_element_type=F32)
 
-    @pl.loop(0, order // 8)
+    @pl.loop(0, order // 8, unroll=2)
     def _(slab):
         transform_in_place(
             mixed, [aligned(pair * order + slab * 8, 8) for pair in range(pairs)]
@@ -203,7 +213,7 @@
 
 
 def pick_kernel(mixed, own_ref, other_ref, out_ref, found, picked):
-    first = lax.axis_index("outer") % 2 == 0
+    first = lax.axis_index("c") == 0
     place = iota((LANES, LANES), 0).astype(F32).astype(BF16)
     row8 = iota((8, LANES), 0)
     one, zero = jnp.ones((), BF16), jnp.zeros((), BF16)
@@ -273,7 +283,7 @@
             for n in range(3):
                 odd = (slot >> (7 + n)) & 1 == 1
                 rows = [jnp.where(odd, b, a) for a, b in zip(rows[0::2], rows[1::2])]
-            picked[aligned(source * CAP + 8 * t, 8), :] = jnp.where(
+            picked[aligned(place_of(source) * CAP + 8 * t, 8), :] = jnp.where(
                 position < count, rows[0] * SCALE, 0.0
             )
 
@@ -368,7 +378,7 @@
 
 def exchange(values):
     values = values.reshape(DEVICES, 1, -1)
-    return lax.all_to_all(values, AXES, split_axis=0, concat_axis=0, tiled=True).reshape(
+    return lax.all_to_all(values, ORDER, split_axis=0, concat_axis=0, tiled=True).reshape(
         -1, LANES
     )
 
@@ -376,8 +386,7 @@
 def per_device(design, sign_bits, sampled, owner_map):
     columns = exchange(local_call(design, sign_bits, sampled, owner_map))
     own = columns.reshape(DEVICES, DATA, LANES)[:, BLOCKS:].reshape(-1, LANES)
-    cores = [(place, place ^ 1) for place in range(lax.axis_size("outer"))]
-    other = lax.ppermute(own, "outer", cores)
+    other = lax.ppermute(own, "c", [(0, 1), (1, 0)])
     picked = exchange(pick_call(mix_call(columns), own, other))
     (tiles,) = call(turn_kernel, [DEVICES * CAP], [VMEM], picked)
     return tiles.reshape(1, DEVICES, CAP, COLS)
@@ -391,6 +400,7 @@
         P(AXES, None),
     )
     out_specs = P(AXES, None, None, None)
+    fine = jax.sharding.Mesh(mesh.devices.reshape(SIZES), AXES)
     return jax.shard_map(
-        per_device, mesh=mesh, in_specs=in_specs, out_specs=out_specs, check_vma=False
+        per_device, mesh=fine, in_specs=in_specs, out_specs=out_specs, check_vma=False
     )

time: 119 us -> 116 us (0.975)
  blocking collectives: 96.6 us -> 93.2 us
    all_to_all x2, blocking collectives: 96.6 us -> 93.2 us  [exchange(): lax.all_to_all(values, ORDER, split_axis=0, concat_axis=0, tiled=True)]
where the time goes in v7:
time: 116 us
  blocking collectives  93.2 us (80%)
  Pallas kernels  21.8 us (19%)
    all_to_all x2, blocking collectives, exchange(): lax.all_to_all(values, ORDER, split_axis=0, concat_axis=0, tiled=True)  93.2 us
    pallas_call x4, Pallas kernels, call(): pl.pallas_call(kernel, out_shape=shapes, in_specs=specs, out_specs=[out]...  21.8 us
  transfers between devices with their start and end apart: 1, of which 0 were waited for; matrix products, arithmetic and copies ran while one was open for 0% of the time, Pallas kernels for 2%

profile of v7, /device:TPU:1, one launch (start us, length us, event | category | flops | bytes accessed | tf_op | source)
XLA Modules:
  0.0 116.0 jit_solution(11336240018480330444)
XLA Ops:
  0.0 9.5 %shard_map.46 = f32[9216,128]{1,0:T(8,128)} custom-call(bf16[8192,128]{1,0:T(8,128)(2,1)} %design_hbm.1, s32[64,128]{1,0:T(8,128)} %bitcast.16, s32[1,1024]{1,0:T(1,128)} %bitcast.17, s32[1,1024]{1,0:T(1,128)} %bitcast.18), custom_call_target="tpu_custom_call" | custom-call | tf_op jit(solution)/shard_map/pallas_call | solution.py:321
  9.5 70.2 %all_to_all.10 = f32[128,1,9216]{2,1,0:T(1,128)S(1)} all-to-all(f32[128,1,9216]{2,1,0:T(1,128)} %bitcast.15), channel_id=1, replica_groups=mesh['y'=4,'h'=2,'z'=4,'l'=2,'c'=2] {'y','z','h','l','c'}, dimensions={0} | all-to-all | bytes 9437184 | tf_op jit(solution)/shard_map/all_to_all | solution.py:381
  79.7 1.0 collective-permute-start
  80.7 2.5 %shard_map.47.mixed = f32[8192,128]{1,0:T(8,128)S(1)} custom-call(f32[9216,128]{1,0:T(8,128)S(1)} %bitcast.12), custom_call_target="tpu_custom_call" | custom-call | tf_op jit(solution)/shard_map/pallas_call | solution.py:321
  83.2 0.0 collective-permute-done.other_ref
  83.2 8.4 %shard_map.48 = f32[2048,128]{1,0:T(8,128)S(1)} custom-call(f32[8192,128]{1,0:T(8,128)S(1)} %shard_map.47.mixed, f32[1024,128]{1,0:T(8,128)S(1)} %slice_bitcast_fusion.own_ref, f32[1024,128]{1,0:T(8,128)S(1)} %collective-permute-done.other_ref), custom_call_target="tpu_custom_call" | custom-call | tf_op jit(solution)/shard_map/pallas_call | solution.py:321
  91.6 23.0 %all_to_all.11 = f32[128,1,2048]{2,1,0:T(1,128)S(1)} all-to-all(f32[128,1,2048]{2,1,0:T(1,128)S(1)} %bitcast.14), channel_id=1, replica_groups=mesh['y'=4,'h'=2,'z'=4,'l'=2,'c'=2] {'y','z','h','l','c'}, dimensions={0} | all-to-all | bytes 2097152 | tf_op jit(solution)/shard_map/all_to_all | solution.py:381
  114.6 1.3 %shard_map.49 = f32[2048,128]{1,0:T(8,128)} custom-call(f32[2048,128]{1,0:T(8,128)S(1)} %bitcast.13), custom_call_target="tpu_custom_call" | custom-call | tf_op jit(solution)/shard_map/pallas_call | solution.py:321
  (1 shorter events, 0.0 us)
Async XLA Ops:
  79.7 3.5 %collective-permute-start = (f32[1024,128]{1,0:T(8,128)S(1)}, f32[1024,128]{1,0:T(8,128)S(1)}, u32[]{:S(2)}, u32[]{:S(2)}) collective-permute-start(f32[1024,128]{1,0:T(8,128)S(1)} %slice_bitcast_fusion.own_ref), channel_id=1, source_target_pairs={{0,1},{1,0},{2,3},{3,2},{4,5},{5,4},{6,7},{7,6},{8,9},{9,8},{10,11... | collective-permute-start | bytes 1572872 | tf_op jit(solution)/shard_map/ppermute | solution.py:389

commit v8 on v7

--- a/solution.py
+++ b/solution.py
@@ -22,8 +22,8 @@
 DATA = BLOCKS + TABLE
 SCALE = 1.0 / math.sqrt(SAMPLED * DEVICES)
 PARTS = 8
-GROUP = 16
-BY_LANES = 5
+GROUP = 64
+BY_LANES = 21
 F32 = jnp.float32
 BF16 = jnp.bfloat16
 
@@ -103,7 +103,7 @@
 
 def local_kernel(
     design_hbm, signs_hbm, sampled_hbm, owner_hbm, out_hbm,
-    design, signs, sampled, owners, at_row, named, mixed, turned, out, sems, small_sems, out_sems,
+    design, signs, sampled, owners, at_row, named, mixed, out, sems, small_sems, out_sems,
 ):
     chunk = ROWS // PARTS
     small = [
@@ -122,7 +122,7 @@
         copy.start()
     order = 2 * LANES
     pairs = BLOCKS // 2
-    matrix = sylvester(order, order)
+    matrix16 = sylvester(order, order).astype(BF16)
     for copy in small:
         copy.wait()
     halves = slot_table(sampled[...], owners[...], at_row, named)
@@ -130,24 +130,22 @@
         copies[n].wait()
         for pair in range(n * pairs // PARTS, (n + 1) * pairs // PARTS):
             sign = (2 * signs[2 * pair : 2 * pair + 2, :] - 1).astype(F32)
-            signed = jnp.concatenate(
-                [matrix[:, :LANES] * sign[0:1], matrix[:, LANES:] * sign[1:2]], axis=1
-            ).astype(BF16)
+            sign16 = jnp.concatenate(
+                [jnp.broadcast_to(sign[t : t + 1], (16, LANES)).astype(BF16) for t in range(2)],
+                axis=1,
+            )[:1]
             rows = pl.ds(pair * order, order)
-            mixed[rows, :] = jnp.dot(signed, design[rows, :], preferred_element_type=F32)
+            result = jnp.dot(
+                design[rows, :].T * sign16, matrix16, preferred_element_type=F32
+            )
+            for t in range(2):
+                place = (t * pairs + pair) * COLS
+                mixed[place : place + COLS, :] = result[:, t * LANES : (t + 1) * LANES]
 
     @pl.loop(0, order // 8, unroll=2)
     def _(slab):
-        transform_in_place(
-            mixed, [aligned(pair * order + slab * 8, 8) for pair in range(pairs)]
-        )
-
-    for t in range(2):
-        for pair in range(pairs):
-            place = t * pairs + pair
-            turned[place * LANES : (place + 1) * LANES, :] = mixed[
-                (2 * pair + t) * LANES : (2 * pair + t + 1) * LANES, :
-            ].T
+        first = (slab // 16) * (pairs * COLS) + (slab % 16) * 8
+        transform_in_place(mixed, [aligned(first + pair * COLS, 8) for pair in range(pairs)])
 
     columns = COLS // PARTS
 
@@ -161,7 +159,7 @@
             for first in range(0, columns, 8):
                 tile = jnp.stack(
                     [
-                        turned[aligned((part * 8 + n) * COLS + step * columns + first, 8), :]
+                        mixed[aligned((part * 8 + n) * COLS + step * columns + first, 8), :]
                         for n in range(8)
                     ]
                 )
@@ -305,11 +303,19 @@
         ].T
 
 
-def turn_kernel(arrived_ref, out_ref):
+def turn_kernel(arrived_ref, out_hbm, out, sems):
+    copies = []
     for group in range(CAP):
-        out_ref[group * LANES : (group + 1) * LANES, :] = arrived_ref[
-            pl.ds(group, COLS, stride=CAP), :
-        ].T
+        rows = pl.ds(group * LANES, LANES)
+        out[rows, :] = arrived_ref[pl.ds(group, COLS, stride=CAP), :].T
+        if group % 4 == 3:
+            rows = pl.ds((group - 3) * LANES, 4 * LANES)
+            copies.append(
+                pltpu.make_async_copy(out.at[rows], out_hbm.at[rows], sems.at[group // 4])
+            )
+            copies[-1].start()
+    for copy in copies:
+        copy.wait()
 
 
 HBM = pl.BlockSpec(memory_space=pltpu.HBM)
@@ -346,7 +352,6 @@
             vmem((DEVICES, SAMPLED), F32),
             vmem((DEVICES, SAMPLED), F32),
             vmem((ROWS, LANES), F32),
-            vmem((ROWS, LANES), F32),
             vmem((COLS * DATA, LANES), F32),
             dma((PARTS,)),
             dma((3,)),
@@ -388,7 +393,14 @@
     own = columns.reshape(DEVICES, DATA, LANES)[:, BLOCKS:].reshape(-1, LANES)
     other = lax.ppermute(own, "c", [(0, 1), (1, 0)])
     picked = exchange(pick_call(mix_call(columns), own, other))
-    (tiles,) = call(turn_kernel, [DEVICES * CAP], [VMEM], picked)
+    (tiles,) = call(
+        turn_kernel,
+        [DEVICES * CAP],
+        [VMEM],
+        picked,
+        scratch=[pltpu.VMEM((DEVICES * CAP, LANES), F32), pltpu.SemaphoreType.DMA((4,))],
+        out=HBM,
+    )
     return tiles.reshape(1, DEVICES, CAP, COLS)
 
 

time: 116 us -> 114 us (0.983)
  Pallas kernels: 21.8 us -> 19.2 us
    pallas_call x4, Pallas kernels: 21.8 us -> 19.2 us  [call(): pl.pallas_call(kernel, out_shape=shapes, in_specs=specs, out_specs=[out]...]
where the time goes in v8:
time: 114 us; the launch traced here: 113 us
  blocking collectives  93.2 us (82%)
  Pallas kernels  19.2 us (17%)
    all_to_all x2, blocking collectives, exchange(): lax.all_to_all(values, ORDER, split_axis=0, concat_axis=0, tiled=True)  93.2 us
    pallas_call x4, Pallas kernels, call(): pl.pallas_call(kernel, out_shape=shapes, in_specs=specs, out_specs=[out]...  19.2 us
  transfers between devices with their start and end apart: 1, of which 0 were waited for; matrix products, arithmetic and copies ran while one was open for 0% of the time, Pallas kernels for 2%

profile of v8, /device:TPU:1, one launch (start us, length us, event | category | flops | bytes accessed | tf_op | source)
XLA Modules:
  0.0 113.4 jit_solution(2894926965291561715)
XLA Ops:
  0.0 8.4 %shard_map.46 = f32[9216,128]{1,0:T(8,128)} custom-call(bf16[8192,128]{1,0:T(8,128)(2,1)} %design_hbm.1, s32[64,128]{1,0:T(8,128)} %bitcast.16, s32[1,1024]{1,0:T(1,128)} %bitcast.17, s32[1,1024]{1,0:T(1,128)} %bitcast.18), custom_call_target="tpu_custom_call" | custom-call | tf_op jit(solution)/shard_map/pallas_call | solution.py:327
  8.4 70.2 %all_to_all.10 = f32[128,1,9216]{2,1,0:T(1,128)S(1)} all-to-all(f32[128,1,9216]{2,1,0:T(1,128)} %bitcast.15), channel_id=1, replica_groups=mesh['y'=4,'h'=2,'z'=4,'l'=2,'c'=2] {'y','z','h','l','c'}, dimensions={0} | all-to-all | bytes 9437184 | tf_op jit(solution)/shard_map/all_to_all | solution.py:386
  78.6 1.0 collective-permute-start
  79.5 2.5 %shard_map.47.mixed = f32[8192,128]{1,0:T(8,128)S(1)} custom-call(f32[9216,128]{1,0:T(8,128)S(1)} %bitcast.12), custom_call_target="tpu_custom_call" | custom-call | tf_op jit(solution)/shard_map/pallas_call | solution.py:327
  82.1 0.0 collective-permute-done.other_ref
  82.1 7.2 %shard_map.48 = f32[2048,128]{1,0:T(8,128)S(1)} custom-call(f32[8192,128]{1,0:T(8,128)S(1)} %shard_map.47.mixed, f32[1024,128]{1,0:T(8,128)S(1)} %slice_bitcast_fusion.own_ref, f32[1024,128]{1,0:T(8,128)S(1)} %collective-permute-done.other_ref), custom_call_target="tpu_custom_call" | custom-call | tf_op jit(solution)/shard_map/pallas_call | solution.py:327
  89.3 23.0 %all_to_all.11 = f32[128,1,2048]{2,1,0:T(1,128)S(1)} all-to-all(f32[128,1,2048]{2,1,0:T(1,128)S(1)} %bitcast.14), channel_id=1, replica_groups=mesh['y'=4,'h'=2,'z'=4,'l'=2,'c'=2] {'y','z','h','l','c'}, dimensions={0} | all-to-all | bytes 2097152 | tf_op jit(solution)/shard_map/all_to_all | solution.py:386
  112.3 1.1 %shard_map.49 = f32[2048,128]{1,0:T(8,128)} custom-call(f32[2048,128]{1,0:T(8,128)S(1)} %bitcast.13), custom_call_target="tpu_custom_call" | custom-call | tf_op jit(solution)/shard_map/pallas_call | solution.py:327
  (1 shorter events, 0.0 us)
Async XLA Ops:
  78.6 3.5 %collective-permute-start = (f32[1024,128]{1,0:T(8,128)S(1)}, f32[1024,128]{1,0:T(8,128)S(1)}, u32[]{:S(2)}, u32[]{:S(2)}) collective-permute-start(f32[1024,128]{1,0:T(8,128)S(1)} %slice_bitcast_fusion.own_ref), channel_id=1, source_target_pairs={{0,1},{1,0},{2,3},{3,2},{4,5},{5,4},{6,7},{7,6},{8,9},{9,8},{10,11... | collective-permute-start | bytes 1572872 | tf_op jit(solution)/shard_map/ppermute | solution.py:394

commit v9 on v8

--- a/solution.py
+++ b/solution.py
@@ -21,7 +21,7 @@
 TABLE = 8
 DATA = BLOCKS + TABLE
 SCALE = 1.0 / math.sqrt(SAMPLED * DEVICES)
-PARTS = 8
+PARTS = 2
 GROUP = 64
 BY_LANES = 21
 F32 = jnp.float32

time: 114 us -> 112 us (0.982)
  Pallas kernels: 19.2 us -> 18 us
    pallas_call x4, Pallas kernels: 19.2 us -> 18 us  [call(): pl.pallas_call(kernel, out_shape=shapes, in_specs=specs, out_specs=[out]...]
where the time goes in v9:
time: 112 us
  blocking collectives  93.2 us (83%)
  Pallas kernels  18 us (16%)
    all_to_all x2, blocking collectives, exchange(): lax.all_to_all(values, ORDER, split_axis=0, concat_axis=0, tiled=True)  93.2 us
    pallas_call x4, Pallas kernels, call(): pl.pallas_call(kernel, out_shape=shapes, in_specs=specs, out_specs=[out]...  18 us
  transfers between devices with their start and end apart: 1, of which 0 were waited for; matrix products, arithmetic and copies ran while one was open for 0% of the time, Pallas kernels for 2%

profile of v9, /device:TPU:1, one launch (start us, length us, event | category | flops | bytes accessed | tf_op | source)
XLA Modules:
  0.0 112.2 jit_solution(11763827974032805856)
XLA Ops:
  0.0 7.1 %shard_map.46 = f32[9216,128]{1,0:T(8,128)} custom-call(bf16[8192,128]{1,0:T(8,128)(2,1)} %design_hbm.1, s32[64,128]{1,0:T(8,128)} %bitcast.16, s32[1,1024]{1,0:T(1,128)} %bitcast.17, s32[1,1024]{1,0:T(1,128)} %bitcast.18), custom_call_target="tpu_custom_call" | custom-call | tf_op jit(solution)/shard_map/pallas_call | solution.py:327
  7.1 70.2 %all_to_all.10 = f32[128,1,9216]{2,1,0:T(1,128)S(1)} all-to-all(f32[128,1,9216]{2,1,0:T(1,128)} %bitcast.15), channel_id=1, replica_groups=mesh['y'=4,'h'=2,'z'=4,'l'=2,'c'=2] {'y','z','h','l','c'}, dimensions={0} | all-to-all | bytes 9437184 | tf_op jit(solution)/shard_map/all_to_all | solution.py:386
  77.3 1.0 collective-permute-start
  78.3 2.5 %shard_map.47.mixed = f32[8192,128]{1,0:T(8,128)S(1)} custom-call(f32[9216,128]{1,0:T(8,128)S(1)} %bitcast.12), custom_call_target="tpu_custom_call" | custom-call | tf_op jit(solution)/shard_map/pallas_call | solution.py:327
  80.8 0.0 collective-permute-done.other_ref
  80.8 7.2 %shard_map.48 = f32[2048,128]{1,0:T(8,128)S(1)} custom-call(f32[8192,128]{1,0:T(8,128)S(1)} %shard_map.47.mixed, f32[1024,128]{1,0:T(8,128)S(1)} %slice_bitcast_fusion.own_ref, f32[1024,128]{1,0:T(8,128)S(1)} %collective-permute-done.other_ref), custom_call_target="tpu_custom_call" | custom-call | tf_op jit(solution)/shard_map/pallas_call | solution.py:327
  88.0 23.0 %all_to_all.11 = f32[128,1,2048]{2,1,0:T(1,128)S(1)} all-to-all(f32[128,1,2048]{2,1,0:T(1,128)S(1)} %bitcast.14), channel_id=1, replica_groups=mesh['y'=4,'h'=2,'z'=4,'l'=2,'c'=2] {'y','z','h','l','c'}, dimensions={0} | all-to-all | bytes 2097152 | tf_op jit(solution)/shard_map/all_to_all | solution.py:386
  111.1 1.1 %shard_map.49 = f32[2048,128]{1,0:T(8,128)} custom-call(f32[2048,128]{1,0:T(8,128)S(1)} %bitcast.13), custom_call_target="tpu_custom_call" | custom-call | tf_op jit(solution)/shard_map/pallas_call | solution.py:327
  (1 shorter events, 0.0 us)
Async XLA Ops:
  77.3 3.5 %collective-permute-start = (f32[1024,128]{1,0:T(8,128)S(1)}, f32[1024,128]{1,0:T(8,128)S(1)}, u32[]{:S(2)}, u32[]{:S(2)}) collective-permute-start(f32[1024,128]{1,0:T(8,128)S(1)} %slice_bitcast_fusion.own_ref), channel_id=1, source_target_pairs={{0,1},{1,0},{2,3},{3,2},{4,5},{5,4},{6,7},{7,6},{8,9},{9,8},{10,11... | collective-permute-start | bytes 1572872 | tf_op jit(solution)/shard_map/ppermute | solution.py:394
